TPU v7x, 32 devices: a whole 2x2x4 slice. The times are simulated.
32 devices in a mesh: dp: 8 (over y, x, core), tensor: 4 (over z).
Axes of the slice: x: 2, y: 2, z: 4, core: 2. Of those that a mesh axis runs over, the one named last changes fastest.
Arguments:
- token_states: bfloat16 [8192, 2048], P('dp', 'tensor'), may hold values from -6 to 6
- norm_gain: bfloat16 [2048], replicated, may hold values from 0.099609375 to 1.8984375
- gate_weight: bfloat16 [2048, 8192], P('dp', 'tensor'), may hold values from -0.125 to 0.125
- up_weight: bfloat16 [2048, 8192], P('dp', 'tensor'), may hold values from -0.125 to 0.125
- down_weight: bfloat16 [8192, 2048], P('tensor', 'dp'), may hold values from -0.0625 to 0.0625
- embed_weight: bfloat16 [2048, 1024], P('tensor'), may hold values from -1 to 1
- text_owner: int32 [128, 1], P('dp'), may hold values from 0 to 7; in each aligned block of 16 rows (0 to 15, 16 to 31, ...) at most 2 rows name the same one
- text_row: int32 [128], P('dp'), may hold values from 0 to 511
- node_cache: bfloat16 [4096, 1024], P('dp', 'tensor'), may hold values from -6 to 6
- tile_index: int32 [32, 6], P('dp'), may hold values from 0 to 7
- tile_live: int32 [32, 6], P('dp'), may hold values 0 or 1
- tile_weight: bfloat16 [32, 6, 128, 128], P('dp'), may hold values from -0.21875 to 0.21875
- self_weight: bfloat16 [1024, 1024], P(None, 'tensor'), may hold values from -0.1875 to 0.1875
- neighbour_weight: bfloat16 [1024, 1024], P(None, 'tensor'), may hold values from -0.1875 to 0.1875
Outputs:
- node_states: bfloat16 [4096, 1024], P('dp', 'tensor')
Inputs may be any that keep to these rules, and one draw needn't show every extreme that they name: `text_owner`: among the 16 texts of one index of dp, at most 2 name the same partition.
All inputs are finite; a program needn't handle non-finite values. No bound on the sum of `tile_live` on one device may be relied on, other than what follows from the above.
Results may differ from a plain program's by a relative error of at most 0.0095.
Values may be sent and summed in bfloat16 or wider, within the bound.
A program may use at most 128 MiB of HBM per device.

v0:
```python
import jax
import jax.numpy as jnp
from jax import lax
from jax.sharding import PartitionSpec as P

CAP = 2
TILE = 128
BT = 2
LAYERS = 2


eps = 1e-05


def with_halo(block, sides, width):
    for axis, dim in sides:
        count = lax.axis_size(axis)
        forward = [(i, i + 1) for i in range(count - 1)]
        backward = [(target, source) for source, target in forward]
        low = lax.ppermute(
            lax.slice_in_dim(block, block.shape[dim] - width, None, axis=dim), axis, forward
        )
        high = lax.ppermute(lax.slice_in_dim(block, 0, width, axis=dim), axis, backward)
        block = jnp.concatenate([low, block, high], axis=dim)
    return block


def per_device(
    token_states,
    norm_gain,
    gate_weight,
    up_weight,
    down_weight,
    embed_weight,
    text_owner,
    text_row,
    node_cache,
    tile_index,
    tile_live,
    tile_weight,
    self_weight,
    neighbour_weight,
):
    text_count = text_row.shape[0]
    owner_list = text_owner[:, 0]
    length = token_states.shape[0] // text_count
    local_width = token_states.shape[1]
    whole = lax.all_gather(token_states, "tensor", axis=1, tiled=True)
    wide = whole.astype(jnp.float32)
    square = jnp.mean(wide * wide, axis=1, keepdims=True)
    normed = (wide * lax.rsqrt(square + eps) * norm_gain.astype(jnp.float32)).astype(jnp.bfloat16)
    gate = jnp.dot(
        normed,
        lax.all_gather(gate_weight, "dp", axis=0, tiled=True),
        preferred_element_type=jnp.float32,
    )
    upward = jnp.dot(
        normed,
        lax.all_gather(up_weight, "dp", axis=0, tiled=True),
        preferred_element_type=jnp.float32,
    )
    hidden = (jax.nn.silu(gate) * upward).astype(jnp.bfloat16)
    own_states = token_states.astype(jnp.float32).reshape(text_count, length, local_width)
    terms = jnp.dot(
        hidden,
        lax.all_gather(down_weight, "dp", axis=1, tiled=True),
        preferred_element_type=jnp.float32,
    )
    down = lax.psum_scatter(
        terms.astype(jnp.bfloat16), "tensor", scatter_dimension=1, tiled=True
    ).astype(jnp.float32)
    pooled = jnp.mean(own_states + down.reshape(text_count, length, local_width), axis=1)
    partial_sum = jnp.dot(pooled, embed_weight.astype(jnp.float32), precision=lax.Precision.HIGHEST)
    fresh = lax.psum_scatter(partial_sum, "tensor", scatter_dimension=1, tiled=True).astype(
        jnp.bfloat16
    )
    node_count = node_cache.shape[0]
    places = jnp.arange(node_count, dtype=jnp.int32)
    groups = lax.axis_size("dp")
    order = jnp.arange(text_count, dtype=jnp.int32)
    earlier = (owner_list[:, None] == owner_list[None, :]) & (order[None, :] < order[:, None])
    rank = jnp.sum(earlier.astype(jnp.int32), axis=1)
    target = owner_list * CAP + rank
    slots = jnp.arange(groups * CAP, dtype=jnp.int32)
    onehot = target[:, None] == slots[None, :]
    sent = jnp.dot(onehot.astype(jnp.bfloat16).T, fresh, preferred_element_type=jnp.float32).astype(
        jnp.bfloat16
    )
    sent_rows = jnp.sum(jnp.where(onehot, text_row[:, None] + 1, 0), axis=0) - 1
    got, got_rows = (
        lax.all_to_all(
            sent.reshape(groups, CAP, -1), "dp", split_axis=0, concat_axis=0, tiled=True
        ),
        lax.all_to_all(
            sent_rows.reshape(groups, CAP), "dp", split_axis=0, concat_axis=0, tiled=True
        ),
    )
    hits = places[:, None] == got_rows.reshape(-1)[None, :]
    added = jnp.dot(
        hits.astype(jnp.bfloat16), got.reshape(groups * CAP, -1), preferred_element_type=jnp.float32
    )
    states = (node_cache.astype(jnp.float32) + added).astype(jnp.bfloat16)
    weights = tile_weight * tile_live.astype(jnp.bfloat16)[:, :, None, None]
    for layer in range(LAYERS):
        gathered = lax.all_gather(states, "tensor", axis=1, tiled=True)
        own_part = jnp.dot(gathered, self_weight, preferred_element_type=jnp.float32)
        projected = jnp.dot(gathered, neighbour_weight, preferred_element_type=jnp.float32)
        extended = with_halo(projected, (("dp", 0),), BT * TILE)
        tiles = extended.reshape(-1, TILE, extended.shape[1])
        picked = tiles[tile_index]
        near_part = jnp.einsum(
            "rkij,rkjh->rih", weights.astype(jnp.float32), picked, precision=lax.Precision.HIGHEST
        )
        total = own_part + near_part.reshape(node_count, -1)
        states = jax.nn.relu(total).astype(jnp.bfloat16)
    return states


def solution(mesh):
    in_specs = (
        P("dp", "tensor"),
        P(),
        P("dp", "tensor"),
        P("dp", "tensor"),
        P("tensor", "dp"),
        P("tensor", None),
        P("dp", None),
        P("dp"),
        P("dp", "tensor"),
        P("dp", None),
        P("dp", None),
        P("dp", None, None, None),
        P(None, "tensor"),
        P(None, "tensor"),
    )
    out_specs = P("dp", "tensor")
    return jax.shard_map(
        per_device, mesh=mesh, in_specs=in_specs, out_specs=out_specs, check_vma=False
    )
```

profile of v0, /device:TPU:1, one launch (start us, length us, event | category | flops | bytes accessed | tf_op | source)
XLA Modules:
  0.0 503.2 jit_solution(11494330023198787225)
XLA Ops:
  10.1 81.8 %all-gather.7.cloned.1.call-done = bf16[1024,2048]{1,0:T(8,128)(2,1)} async-done(((bf16[1024,512]{1,0:T(8,128)(2,1)}), bf16[1024,2048]{1,0:T(8,128)(2,1)}) %all-gather.7.cloned.1.call-update) | async-done | bytes 4194320 | tf_op jit(solution)/shard_map/all_gather | solution.py:48
  91.8 3.1 fusion
  94.9 52.2 %all-gather.9.cloned.1.call-done = bf16[2048,2048]{1,0:T(8,128)(2,1)} async-done(((bf16[256,2048]{1,0:T(8,128)(2,1)}), bf16[2048,2048]{1,0:T(8,128)(2,1)}) %all-gather.9.cloned.1.call-update) | async-done | bytes 8388624 | tf_op jit(solution)/shard_map/all_gather | solution.py:54
  147.1 14.6 %fusion.10 = f32[1024,2048]{1,0:T(8,128)} fusion(bf16[2048,2048]{1,0:T(8,128)(2,1)} %all-gather.9.cloned.1.call-done, bf16[1024,2048]{1,0:T(8,128)(2,1)} %all-gather.7.cloned.1.call-done, f32[2048]{0:T(1024)S(1)} %convert_element_type.54, f32[1024]{0:T(1024)S(1)} %add_rsqrt_fusion), kind=kOutput, calls=%fused_computation.18 | convolution fusion | flops 8598323200 | bytes 20983808 | tf_op jit(solution)/shard_map/dot_general | solution.py:52
  161.6 41.8 %all-gather.11.cloned.1.call-done = bf16[2048,2048]{1,0:T(8,128)(2,1)} async-done(((bf16[256,2048]{1,0:T(8,128)(2,1)}), bf16[2048,2048]{1,0:T(8,128)(2,1)}) %all-gather.11.cloned.1.call-update) | async-done | bytes 8388624 | tf_op jit(solution)/shard_map/all_gather | solution.py:59
  203.4 57.7 %all-gather.13.cloned.1.call-done = bf16[2048,2048]{1,0:T(8,128)(2,1)} async-done(((bf16[2048,256]{1,0:T(8,128)(2,1)}), bf16[2048,2048]{1,0:T(8,128)(2,1)}) %all-gather.13.cloned.1.call-update) | async-done | bytes 8388624 | tf_op jit(solution)/shard_map/all_gather | solution.py:66
  261.1 27.3 %fusion.5 = bf16[1024,2048]{1,0:T(8,128)(2,1)} fusion(bf16[2048,2048]{1,0:T(8,128)(2,1)} %all-gather.13.cloned.1.call-done, f32[1024,2048]{1,0:T(8,128)} %fusion.10, bf16[2048,2048]{1,0:T(8,128)(2,1)} %all-gather.11.cloned.1.call-done, bf16[1024,2048]{1,0:T(8,128)(2,1)} %all-gather.7.cloned.1.call-done, f32[2048]{0:T(1024)S(1)} %convert_element_type.54, ...), kind=kOutput, calls=%fused_computation.10 | convolution fusion | flops 17202937856 | bytes 33566720 | tf_op jit(solution)/shard_map/dot_general | solution.py:64
  288.8 76.2 %reduce-scatter.3.cloned.1.call-done = bf16[1024,512]{1,0:T(8,128)(2,1)} async-done(((bf16[1024,2048]{1,0:T(8,128)(2,1)}), bf16[1024,512]{1,0:T(8,128)(2,1)}) %reduce-scatter.3.cloned.1.call-update) | async-done | bytes 1048592 | tf_op jit(solution)/shard_map/reduce_scatter | solution.py:69
  368.4 4.3 all-to-all-start
  372.7 12.4 %reduce-scatter.5.cloned.1.call-done = f32[16,256]{1,0:T(8,128)} async-done(((f32[16,1024]{1,0:T(8,128)}), f32[16,256]{1,0:T(8,128)}) %reduce-scatter.5.cloned.1.call-update) | async-done | bytes 16400 | tf_op jit(solution)/shard_map/reduce_scatter | solution.py:74
  386.7 6.5 %all-to-all-start.1 = ((bf16[8,2,256]{2,1,0:T(2,128)(2,1)}), bf16[8,2,256]{2,1,0:T(2,128)(2,1)S(1)}, u32[]{:S(2)}, u32[]{:S(2)}) async-start(bf16[8,2,256]{2,1,0:T(2,128)(2,1)} %reshape.53), calls=%async_computation.3 | async-start | bytes 16384 | tf_op jit(solution)/shard_map/all_to_all | solution.py:91
  394.6 2.7 all-to-all-done.1
  399.2 25.4 %all-gather.15.cloned.1.call-done = bf16[512,1024]{1,0:T(8,128)(2,1)} async-done(((bf16[512,256]{1,0:T(8,128)(2,1)}), bf16[512,1024]{1,0:T(8,128)(2,1)}) %all-gather.15.cloned.1.call-update) | async-done | bytes 1048592 | tf_op jit(solution)/shard_map/all_gather | solution.py:105
  426.3 4.0 collective-permute-start
  434.3 3.8 collective-permute-done.1
  439.2 2.4 gather_fusion
  441.6 3.2 fusion.17
  444.8 2.5 fusion.14
  447.3 27.4 %all-gather.17.cloned.1.call-done = bf16[512,1024]{1,0:T(8,128)(2,1)} async-done(((bf16[512,256]{1,0:T(8,128)(2,1)}), bf16[512,1024]{1,0:T(8,128)(2,1)}) %all-gather.17.cloned.1.call-update) | async-done | bytes 1048592 | tf_op jit(solution)/shard_map/all_gather | solution.py:105
  476.6 4.0 collective-permute-start.2
  483.9 4.4 collective-permute-done.3
  488.4 2.4 gather_fusion.1
  490.8 3.4 fusion.15
  494.2 2.2 fusion.13
  (68 shorter events, 24.1 us)
Async XLA Ops:
  6.5 360.0 %copy-start = (bf16[512,1024]{1,0:T(8,128)(2,1)S(1)}, bf16[512,1024]{1,0:T(8,128)(2,1)}, u32[]{:S(2)}) copy-start(bf16[512,1024]{1,0:T(8,128)(2,1)} %param.19) | copy-start | bytes 3145732
  6.5 85.3 %all-gather.7.cloned.1.call-start = ((), (), s32[]{:S(2)}) async-start(), calls=%async_computation.4 | async-start | bytes 5242880 | tf_op jit(solution)/shard_map/all_gather | solution.py:48
  7.3 139.8 %all-gather.9.cloned.1.call-start = ((), (), s32[]{:S(2)}) async-start(), calls=%async_computation.5 | async-start | bytes 9437184 | tf_op jit(solution)/shard_map/all_gather | solution.py:54
  8.0 195.4 %all-gather.11.cloned.1.call-start = ((), (), s32[]{:S(2)}) async-start(), calls=%async_computation.6 | async-start | bytes 9437184 | tf_op jit(solution)/shard_map/all_gather | solution.py:59
  8.7 252.4 %all-gather.13.cloned.1.call-start = ((), (), s32[]{:S(2)}) async-start(), calls=%async_computation.7 | async-start | bytes 9437184 | tf_op jit(solution)/shard_map/all_gather | solution.py:66
  9.3 355.7 %reduce-scatter.3.cloned.1.call-start = ((), (), s32[]{:S(2)}) async-start(), calls=%async_computation.8 | async-start | bytes 5242880 | tf_op jit(solution)/shard_map/reduce_scatter | solution.py:69
  161.6 126.9 %copy-start.9 = (s32[16,1]{0,1:T(1,128)S(1)}, s32[16,1]{0,1:T(1,128)}, u32[]{:S(2)}) copy-start(s32[16,1]{0,1:T(1,128)} %param.20) | copy-start | bytes 196
  161.6 127.1 %copy-start.8 = (s32[16]{0:T(128)S(1)}, s32[16]{0:T(128)}, u32[]{:S(2)}) copy-start(s32[16]{0:T(128)} %param.21) | copy-start | bytes 196
  161.6 203.4 %copy-start.1 = (bf16[1024,512]{1,0:T(8,128)(2,1)S(1)}, bf16[1024,512]{1,0:T(8,128)(2,1)}, u32[]{:S(2)}) copy-start(bf16[1024,512]{1,0:T(8,128)(2,1)} %param.14) | copy-start | bytes 3145732
  288.4 136.2 %copy-start.4 = (bf16[1024,256]{1,0:T(8,128)(2,1)S(1)}, bf16[1024,256]{1,0:T(8,128)(2,1)}, u32[]{:S(2)}) copy-start(bf16[1024,256]{1,0:T(8,128)(2,1)} %param.27) | copy-start | bytes 1572868
  288.4 143.8 %copy-start.7 = (s32[4,6]{1,0:T(4,128)S(1)}, s32[4,6]{1,0:T(4,128)}, u32[]{:S(2)}) copy-start(s32[4,6]{1,0:T(4,128)} %param.23) | copy-start | bytes 292
  288.4 143.9 %copy-start.6 = (s32[4,6]{1,0:T(4,128)S(1)}, s32[4,6]{1,0:T(4,128)}, u32[]{:S(2)}) copy-start(s32[4,6]{1,0:T(4,128)} %param.24) | copy-start | bytes 292
  288.5 153.2 %copy-start.3 = (bf16[4,6,128,128]{3,2,1,0:T(8,128)(2,1)S(1)}, bf16[4,6,128,128]{3,2,1,0:T(8,128)(2,1)}, u32[]{:S(2)}) copy-start(bf16[4,6,128,128]{3,2,1,0:T(8,128)(2,1)} %param.25) | copy-start | bytes 2359300
  288.5 96.7 %reduce-scatter.5.cloned.1.call-start = ((), (), s32[]{:S(2)}) async-start(), calls=%async_computation.9 | async-start | bytes 81920 | tf_op jit(solution)/shard_map/reduce_scatter | solution.py:74
  368.4 18.3 %all-to-all-start = ((s32[8,1,2]{2,1,0:T(1,128)}), s32[8,1,2]{2,1,0:T(1,128)S(1)}, u32[]{:S(2)}, u32[]{:S(2)}) async-start(s32[8,1,2]{2,1,0:T(1,128)} %bitcast.3), calls=%async_computation | async-start | bytes 8192 | tf_op jit(solution)/shard_map/all_to_all | solution.py:94
  386.7 10.5 %all-to-all-start.1 = ((bf16[8,2,256]{2,1,0:T(2,128)(2,1)}), bf16[8,2,256]{2,1,0:T(2,128)(2,1)S(1)}, u32[]{:S(2)}, u32[]{:S(2)}) async-start(bf16[8,2,256]{2,1,0:T(2,128)(2,1)} %reshape.53), calls=%async_computation.3 | async-start | bytes 16384 | tf_op jit(solution)/shard_map/all_to_all | solution.py:91
  393.3 31.3 %all-gather.15.cloned.1.call-start = ((), (), s32[]{:S(2)}) async-start(), calls=%async_computation.10 | async-start | bytes 1310720 | tf_op jit(solution)/shard_map/all_gather | solution.py:105
  399.2 75.5 %all-gather.17.cloned.1.call-start = ((), (), s32[]{:S(2)}) async-start(), calls=%async_computation.11 | async-start | bytes 1310720 | tf_op jit(solution)/shard_map/all_gather | solution.py:105
  426.3 7.3 %collective-permute-start = (f32[256,256]{1,0:T(8,128)S(1)}, f32[256,256]{1,0:T(8,128)S(1)}, u32[]{:S(2)}, u32[]{:S(2)}) collective-permute-start(f32[256,256]{1,0:T(8,128)S(1)} %get-tuple-element.7), channel_id=1, source_target_pairs={{0,4},{4,8},{8,12},{12,16},{16,20},{20,24},{24,28},{1,5},{5,9},{9,... | collective-permute-start | bytes 786440 | tf_op jit(solution)/shard_map/ppermute | solution.py:20
  430.3 7.8 %collective-permute-start.1 = (f32[256,256]{1,0:T(8,128)S(1)}, f32[256,256]{1,0:T(8,128)}, u32[]{:S(2)}, u32[]{:S(2)}) collective-permute-start(f32[256,256]{1,0:T(8,128)S(1)} %get-tuple-element.8), channel_id=1, source_target_pairs={{4,0},{8,4},{12,8},{16,12},{20,16},{24,20},{28,24},{5,1},{9,5},{13... | collective-permute-start | bytes 786440 | tf_op jit(solution)/shard_map/ppermute | solution.py:23
  433.6 0.7 copy-start.5
  474.7 19.5 %copy-start.2 = (bf16[512,1024]{1,0:T(8,128)(2,1)S(1)}, bf16[512,1024]{1,0:T(8,128)(2,1)}, u32[]{:S(2)}) copy-start(bf16[512,1024]{1,0:T(8,128)(2,1)} %all-gather.17.cloned.1.call-done) | copy-start | bytes 3145732
  476.6 7.3 %collective-permute-start.2 = (f32[256,256]{1,0:T(8,128)S(1)}, f32[256,256]{1,0:T(8,128)S(1)}, u32[]{:S(2)}, u32[]{:S(2)}) collective-permute-start(f32[256,256]{1,0:T(8,128)S(1)} %get-tuple-element.5), channel_id=1, source_target_pairs={{0,4},{4,8},{8,12},{12,16},{16,20},{20,24},{24,28},{1,5},{5,9},{9,... | collective-permute-start | bytes 786440 | tf_op jit(solution)/shard_map/ppermute | solution.py:20
  480.6 7.7 %collective-permute-start.3 = (f32[256,256]{1,0:T(8,128)S(1)}, f32[256,256]{1,0:T(8,128)S(1)}, u32[]{:S(2)}, u32[]{:S(2)}) collective-permute-start(f32[256,256]{1,0:T(8,128)S(1)} %get-tuple-element.6), channel_id=1, source_target_pairs={{4,0},{8,4},{12,8},{16,12},{20,16},{24,20},{28,24},{5,1},{9,5},{13... | collective-permute-start | bytes 786440 | tf_op jit(solution)/shard_map/ppermute | solution.py:23
Sparse Core Ops, SparseCore 0:
  8.9 82.8 all-gather.6
  93.7 53.3 all-gather.8
  149.0 54.3 all-gather.10
  205.1 55.9 all-gather.12
  288.6 76.3 reduce-scatter.2
  367.9 17.2 reduce-scatter.4
  399.3 25.2 all-gather.14
  447.5 27.1 all-gather.16
where the time goes:
time: 504 us; the launch traced here: 503 us
  waiting for transfers between devices  391 us (78%)
  matrix products  60.7 us (12%)
  starting transfers between devices  22.8 us (5%)
  between operations  13.7 us (3%)
  local copies, waits for them, and re-layouts  7.62 us (2%)
  other arithmetic  7.43 us (1%)
    all_gather x1, waiting for transfers between devices, per_device(): whole = lax.all_gather(token_states, 'tensor', axis=1, tiled=True)  81.8 us
    reduce_scatter x1, waiting for transfers between devices, per_device(): lax.psum_scatter(terms.astype(jnp.bfloat16), 'tensor', scatter_dimension=...  76.2 us
    all_gather x1, waiting for transfers between devices, per_device(): lax.all_gather(down_weight, 'dp', axis=1, tiled=True)  57.7 us
    all_gather x2, waiting for transfers between devices, per_device(): gathered = lax.all_gather(states, 'tensor', axis=1, tiled=True)  52.7 us
    all_gather x1, waiting for transfers between devices, per_device(): lax.all_gather(gate_weight, 'dp', axis=0, tiled=True)  52.2 us
    all_gather x1, waiting for transfers between devices, per_device(): lax.all_gather(up_weight, 'dp', axis=0, tiled=True)  41.8 us
    dot_general x1, matrix products, per_device(): jnp.dot(hidden, lax.all_gather(down_weight, 'dp', axis=1, tiled=True), pr...  27.3 us
    dot_general x1, matrix products, per_device(): jnp.dot(normed, lax.all_gather(gate_weight, 'dp', axis=0, tiled=True), pr...  14.6 us
  transfers between devices with their start and end apart: 14, of which 13 were waited for; matrix products, arithmetic and copies ran while one was open for 4% of the time, Pallas kernels for 0%

commit v1 on v0

v1 whole, which is shorter than its diff:
```python
import jax
import jax.numpy as jnp
from jax import lax
from jax.sharding import PartitionSpec as P

TILE = 128
BT = 2
LAYERS = 2

eps = 1e-05
f32 = jnp.float32
bf16 = jnp.bfloat16


def exchange(block, axis):
    return lax.all_to_all(block, axis, split_axis=0, concat_axis=0, tiled=True)


def spread(block, axis):
    count = lax.axis_size(axis)
    return exchange(jnp.broadcast_to(block[None], (count,) + block.shape), axis)


def with_halo(block, width):
    count = lax.axis_size("dp")
    forward = [(i, i + 1) for i in range(count - 1)]
    backward = [(target, source) for source, target in forward]
    low = lax.ppermute(block[block.shape[0] - width :], "dp", forward)
    high = lax.ppermute(block[:width], "dp", backward)
    return jnp.concatenate([low, block, high], axis=0)


def side_by_side(blocks):
    return jnp.concatenate([blocks[i] for i in range(blocks.shape[0])], axis=1)


def pooled_hidden(token_states, norm_gain, gate_weight, up_weight, length):
    whole = side_by_side(spread(token_states, "tensor"))
    wide = whole.astype(f32)
    square = jnp.mean(wide * wide, axis=1, keepdims=True)
    normed = (wide * lax.rsqrt(square + eps) * norm_gain.astype(f32)).astype(bf16)
    gate = jnp.dot(
        normed,
        lax.all_gather(gate_weight, "dp", axis=0, tiled=True),
        preferred_element_type=f32,
    )
    upward = jnp.dot(
        normed,
        lax.all_gather(up_weight, "dp", axis=0, tiled=True),
        preferred_element_type=f32,
    )
    hidden = (jax.nn.silu(gate) * upward).astype(bf16)
    return jnp.mean(hidden.astype(f32).reshape(-1, length, hidden.shape[1]), axis=1)


def per_device(
    token_states,
    norm_gain,
    gate_weight,
    up_weight,
    down_weight,
    embed_weight,
    text_owner,
    text_row,
    node_cache,
    tile_index,
    tile_live,
    tile_weight,
    self_weight,
    neighbour_weight,
):
    groups, parts = lax.axis_size("dp"), lax.axis_size("tensor")
    me, col = lax.axis_index("dp"), lax.axis_index("tensor")
    text_count = text_row.shape[0]
    texts = text_count * groups
    length = token_states.shape[0] // text_count
    node_count = node_cache.shape[0]
    halo = BT * TILE

    cache = side_by_side(spread(with_halo(node_cache, halo), "tensor"))
    row_tiles, slots = tile_index.shape
    columns = row_tiles + 2 * BT
    live = (tile_index[:, :, None] == jnp.arange(columns)[None, None, :]) & (
        tile_live[:, :, None] != 0
    )
    adjacency = jnp.zeros((row_tiles, TILE, columns, TILE), f32)
    for slot in range(slots):
        adjacency += jnp.where(
            live[:, slot, None, :, None], tile_weight[:, slot, :, None, :].astype(f32), 0.0
        )
    adjacency = adjacency.astype(bf16).reshape(row_tiles * TILE, columns * TILE)
    place = text_owner[:, 0] * node_count + text_row
    places = spread(place, "dp").reshape(-1)
    width = down_weight.shape[1]
    whole_embed = lax.all_gather(embed_weight, "tensor", axis=0, tiled=True)
    own_embed = lax.dynamic_slice_in_dim(whole_embed, me * width, width, axis=0)
    token_mean = jnp.mean(
        token_states.astype(f32).reshape(text_count, length, -1), axis=1
    )

    mean_hidden = pooled_hidden(token_states, norm_gain, gate_weight, up_weight, length)

    hidden_all = spread(mean_hidden.astype(bf16), "dp").reshape(texts, -1)
    share = jnp.dot(hidden_all, down_weight, preferred_element_type=f32)
    rows = texts // parts
    part = jnp.sum(exchange(share.reshape(parts, rows, width), "tensor"), axis=0)
    pooled = jnp.dot(part, own_embed.astype(f32), precision=lax.Precision.HIGHEST)
    fine = rows // groups
    pooled = jnp.sum(exchange(pooled.reshape(groups, fine, -1), "dp"), axis=0)
    direct = jnp.dot(token_mean, embed_weight.astype(f32), precision=lax.Precision.HIGHEST)
    direct = spread(direct, "dp").reshape(parts, rows, -1)
    direct = jnp.sum(exchange(direct, "tensor"), axis=0)
    direct = lax.dynamic_slice_in_dim(direct, me * fine, fine, axis=0)
    fresh = (pooled + direct).astype(bf16)
    fresh = spread(spread(fresh, "dp").reshape(rows, -1), "tensor").reshape(texts, -1)

    ahead = me * node_count - halo + jnp.arange(cache.shape[0], dtype=jnp.int32)
    hits = (ahead[:, None] == places[None, :]).astype(bf16)
    added = jnp.dot(hits, fresh, preferred_element_type=f32)
    extended = (cache.astype(f32) + added).astype(bf16)
    gathered = extended[halo : halo + node_count]
    for layer in range(LAYERS):
        if layer > 0:
            gathered = side_by_side(spread(states, "tensor"))
            projected = jnp.dot(gathered, neighbour_weight, preferred_element_type=f32)
            projected = with_halo(projected.astype(bf16), halo)
        else:
            projected = jnp.dot(extended, neighbour_weight, preferred_element_type=f32)
            projected = projected.astype(bf16)
        own_part = jnp.dot(gathered, self_weight, preferred_element_type=f32)
        near_part = jnp.dot(adjacency, projected, preferred_element_type=f32)
        states = jax.nn.relu(own_part + near_part).astype(bf16)
    return states


def solution(mesh):
    in_specs = (
        P("dp", "tensor"),
        P(),
        P("dp", "tensor"),
        P("dp", "tensor"),
        P("tensor", "dp"),
        P("tensor", None),
        P("dp", None),
        P("dp"),
        P("dp", "tensor"),
        P("dp", None),
        P("dp", None),
        P("dp", None, None, None),
        P(None, "tensor"),
        P(None, "tensor"),
    )
    out_specs = P("dp", "tensor")
    return jax.shard_map(
        per_device, mesh=mesh, in_specs=in_specs, out_specs=out_specs, check_vma=False
    )
```

time: 504 us -> 366 us (0.73)
  waiting for transfers between devices: 391 us -> 190 us
  blocking collectives: 0 us -> 42.2 us
  starting transfers between devices: 22.8 us -> 54.3 us
  matrix products: 60.7 us -> 43.6 us
  local copies, waits for them, and re-layouts: 7.62 us -> 15.4 us
    all_gather x6 -> x3, waiting for transfers between devices: 286 us -> 20.4 us  [the longest x1 20.4 us: per_device(): whole_embed = lax.all_gather(embed_weight, 'tensor', axis=0, tiled=True)]
    all_to_all x2 -> x9, waiting for transfers between devices: 2.7 us -> 164 us  [exchange(): return lax.all_to_all(block, axis, split_axis=0, concat_axis=0, tiled=True)]
    reduce_scatter x2 -> x0, waiting for transfers between devices: 88.6 us -> none  [the longest x1 76.2 us: per_device(): lax.psum_scatter(terms.astype(jnp.bfloat16), 'tensor', scatter_dimension=...]
    all_to_all x0 -> x2, blocking collectives: none -> 42.2 us  [exchange(): return lax.all_to_all(block, axis, split_axis=0, concat_axis=0, tiled=True)]
    all_to_all x2 -> x9, starting transfers between devices: 10.8 us -> 40.5 us  [exchange(): return lax.all_to_all(block, axis, split_axis=0, concat_axis=0, tiled=True)]
    dot_general x11, matrix products: 60.7 us -> 43.6 us  [the longest x1 16.6 us: pooled_hidden(): jnp.dot(normed, lax.all_gather(up_weight, 'dp', axis=0, tiled=True), pref...]
    broadcast_in_dim x1 -> x10, local copies, waits for them, and re-layouts: 0.08 us -> 8.82 us  [the longest x9 8.81 us: spread(): return exchange(jnp.broadcast_to(block[None], (count,) + block.shape), axis)]
    ppermute x4, waiting for transfers between devices: 10.9 us -> 3.9 us  [the longest x2 3.9 us: with_halo(): high = lax.ppermute(block[:width], 'dp', backward)]
  transfers between devices with their start and end apart: 14 -> 16, of which waited for: 13 -> 10; matrix products, arithmetic and copies ran while one was open for 4% -> 14% of each run, Pallas kernels for 0% -> 0%
where the time goes in v1:
time: 366 us; the launch traced here: 365 us
  waiting for transfers between devices  190 us (52%)
  starting transfers between devices  54.3 us (15%)
  matrix products  43.6 us (12%)
  blocking collectives  42.2 us (12%)
  local copies, waits for them, and re-layouts  15.4 us (4%)
  between operations  13.6 us (4%)
  other arithmetic  5.28 us (1%)
    all_to_all x9, waiting for transfers between devices, exchange(): return lax.all_to_all(block, axis, split_axis=0, concat_axis=0, tiled=True)  164 us
    all_to_all x2, blocking collectives, exchange(): return lax.all_to_all(block, axis, split_axis=0, concat_axis=0, tiled=True)  42.2 us
    all_to_all x9, starting transfers between devices, exchange(): return lax.all_to_all(block, axis, split_axis=0, concat_axis=0, tiled=True)  40.5 us
    all_gather x1, waiting for transfers between devices, per_device(): whole_embed = lax.all_gather(embed_weight, 'tensor', axis=0, tiled=True)  20.4 us
    dot_general x1, matrix products, pooled_hidden(): jnp.dot(normed, lax.all_gather(up_weight, 'dp', axis=0, tiled=True), pref...  16.6 us
    dot_general x1, matrix products, pooled_hidden(): jnp.dot(normed, lax.all_gather(gate_weight, 'dp', axis=0, tiled=True), pr...  15.2 us
    ppermute x2, starting transfers between devices, with_halo(): low = lax.ppermute(block[block.shape[0] - width:], 'dp', forward)  9.98 us
    broadcast_in_dim x9, local copies, waits for them, and re-layouts, spread(): return exchange(jnp.broadcast_to(block[None], (count,) + block.shape), axis)  8.81 us
  transfers between devices with their start and end apart: 16, of which 10 were waited for; matrix products, arithmetic and copies ran while one was open for 14% of the time, Pallas kernels for 0%

profile of v1, /device:TPU:1, one launch (start us, length us, event | category | flops | bytes accessed | tf_op | source)
XLA Modules:
  0.0 364.9 jit_solution(4287899449237379346)
XLA Ops:
  8.0 3.6 broadcast_in_dim.144
  11.6 5.6 %all-to-all-start.2 = ((bf16[4,1024,512]{2,1,0:T(8,128)(2,1)}), bf16[4,1024,512]{2,1,0:T(8,128)(2,1)}, u32[]{:S(2)}, u32[]{:S(2)}) async-start(bf16[4,1024,512]{2,1,0:T(8,128)(2,1)} %broadcast_in_dim.144), calls=%async_computation.2 | async-start | bytes 8388608 | tf_op jit(solution)/shard_map/all_to_all | solution.py:16
  17.9 92.2 %all-to-all-done.2 = bf16[4,1024,512]{2,1,0:T(8,128)(2,1)} async-done(((bf16[4,1024,512]{2,1,0:T(8,128)(2,1)}), bf16[4,1024,512]{2,1,0:T(8,128)(2,1)}, u32[]{:S(2)}, u32[]{:S(2)}) %all-to-all-start.2) | async-done | bytes 4194336 | tf_op jit(solution)/shard_map/all_to_all | solution.py:16
  114.5 15.2 %fusion.6 = f32[1024,2048]{1,0:T(8,128)} fusion(bf16[2048,2048]{1,0:T(8,128)(2,1)} %all-gather.4.cloned.1.call-done, f32[2048]{0:T(1024)S(1)} %convert_element_type.117, f32[1024]{0:T(1024)S(1)} %add_rsqrt_fusion, bf16[1024,512]{1,0:T(8,128)(2,1)S(1)} %get-tuple-element.6, bf16[1024,512]{1,0:T(8,128)(2,1)} %copy-done.5, bf16[1024,512]{1,0:T(8,128)(2,1)} %copy-done.6, ...), kind=kOutput, calls=%fused_computation.16 | convolution fusion | flops 8613003264 | bytes 20983808 | tf_op jit(solution)/shard_map/dot_general | solution.py:42
  129.7 16.6 %convert_reduce_fusion = f32[16,2048]{1,0:T(8,128)S(1)} fusion(bf16[2048,2048]{1,0:T(8,128)(2,1)} %all-gather.6.cloned.1.call-done, f32[1024,2048]{1,0:T(8,128)} %fusion.6, f32[2048]{0:T(1024)S(1)} %convert_element_type.117, f32[1024]{0:T(1024)S(1)} %add_rsqrt_fusion, bf16[1024,512]{1,0:T(8,128)(2,1)} %copy-done.4, bf16[1024,512]{1,0:T(8,128)(2,1)} %copy-done.5, ...), kind=kOutput, calls=%fused_computation.5 | convolution fusion | flops 8629747712 | bytes 21114880 | tf_op jit(solution)/shard_map/dot_general | solution.py:47
  147.2 5.1 %all-to-all-start.3 = ((bf16[8,16,2048]{2,1,0:T(8,128)(2,1)}), bf16[8,16,2048]{2,1,0:T(8,128)(2,1)}, u32[]{:S(2)}, u32[]{:S(2)}) async-start(bf16[8,16,2048]{2,1,0:T(8,128)(2,1)} %broadcast_in_dim.145), calls=%async_computation.3 | async-start | bytes 1048576 | tf_op jit(solution)/shard_map/all_to_all | solution.py:16
  153.1 6.4 %all-to-all-done.3 = bf16[8,16,2048]{2,1,0:T(8,128)(2,1)} async-done(((bf16[8,16,2048]{2,1,0:T(8,128)(2,1)}), bf16[8,16,2048]{2,1,0:T(8,128)(2,1)}, u32[]{:S(2)}, u32[]{:S(2)}) %all-to-all-start.3) | async-done | bytes 524320 | tf_op jit(solution)/shard_map/all_to_all | solution.py:16
  160.3 6.7 %all-to-all-start.6 = ((f32[8,16,1024]{2,1,0:T(8,128)}), f32[8,16,1024]{2,1,0:T(8,128)}, u32[]{:S(2)}, u32[]{:S(2)}) async-start(f32[8,16,1024]{2,1,0:T(8,128)} %broadcast_in_dim.146), calls=%async_computation.6 | async-start | bytes 1048576 | tf_op jit(solution)/shard_map/all_to_all | solution.py:16
  168.4 5.8 %all-to-all-done.6 = f32[8,16,1024]{2,1,0:T(8,128)} async-done(((f32[8,16,1024]{2,1,0:T(8,128)}), f32[8,16,1024]{2,1,0:T(8,128)}, u32[]{:S(2)}, u32[]{:S(2)}) %all-to-all-start.6) | async-done | bytes 524320 | tf_op jit(solution)/shard_map/all_to_all | solution.py:16
  174.2 12.6 %all_to_all.56 = f32[4,32,256]{2,1,0:T(8,128)S(1)} all-to-all(f32[4,32,256]{2,1,0:T(8,128)S(1)} %fusion.14), channel_id=1, replica_groups=mesh['dp'=8,'tensor'=4] {'tensor'}, dimensions={0} | all-to-all | bytes 262144 | tf_op jit(solution)/shard_map/all_to_all | solution.py:16
  186.8 3.5 all-to-all-start.7
  190.4 5.7 %collective-permute-start = (bf16[256,256]{1,0:T(8,128)(2,1)S(1)}, bf16[256,256]{1,0:T(8,128)(2,1)S(1)}, u32[]{:S(2)}, u32[]{:S(2)}) collective-permute-start(bf16[256,256]{1,0:T(8,128)(2,1)S(1)} %get-tuple-element.25), channel_id=1, source_target_pairs={{0,4},{4,8},{8,12},{12,16},{16,20},{20,24},{24,28},{1,5},{5,9},{9,... | collective-permute-start | bytes 393224 | tf_op jit(solution)/shard_map/ppermute | solution.py:28
  198.0 20.4 %all-gather.8.cloned.1.call-done = bf16[2048,1024]{1,0:T(8,128)(2,1)} async-done(((bf16[512,1024]{1,0:T(8,128)(2,1)}), bf16[2048,1024]{1,0:T(8,128)(2,1)}) %all-gather.8.cloned.1.call-update) | async-done | bytes 4194320 | tf_op jit(solution)/shard_map/all_gather | solution.py:95
  220.5 4.3 %all-to-all-start.5 = ((f32[8,4,1024]{2,1,0:T(4,128)}), f32[8,4,1024]{2,1,0:T(4,128)S(1)}, u32[]{:S(2)}, u32[]{:S(2)}) async-start(f32[8,4,1024]{2,1,0:T(4,128)} %fusion.23), calls=%async_computation.5 | async-start | bytes 262144 | tf_op jit(solution)/shard_map/all_to_all | solution.py:16
  224.9 4.6 %all-to-all-done.5 = f32[8,4,1024]{2,1,0:T(4,128)S(1)} async-done(((f32[8,4,1024]{2,1,0:T(4,128)}), f32[8,4,1024]{2,1,0:T(4,128)S(1)}, u32[]{:S(2)}, u32[]{:S(2)}) %all-to-all-start.5) | async-done | bytes 131104 | tf_op jit(solution)/shard_map/all_to_all | solution.py:16
  230.0 4.1 %all-to-all-start.1 = ((s32[8,1,16]{2,1,0:T(1,128)}), s32[8,1,16]{2,1,0:T(1,128)S(1)}, u32[]{:S(2)}, u32[]{:S(2)}) async-start(s32[8,1,16]{2,1,0:T(1,128)} %broadcast_in_dim.143), calls=%async_computation.1 | async-start | bytes 8192 | tf_op jit(solution)/shard_map/all_to_all | solution.py:16
  234.2 3.9 %all-to-all-done.1 = s32[8,1,16]{2,1,0:T(1,128)S(1)} async-done(((s32[8,1,16]{2,1,0:T(1,128)}), s32[8,1,16]{2,1,0:T(1,128)S(1)}, u32[]{:S(2)}, u32[]{:S(2)}) %all-to-all-start.1) | async-done | bytes 544 | tf_op jit(solution)/shard_map/all_to_all | solution.py:16
  238.7 4.0 %all-to-all-start.8 = ((bf16[8,4,1024]{2,1,0:T(4,128)(2,1)}), bf16[8,4,1024]{2,1,0:T(4,128)(2,1)S(1)}, u32[]{:S(2)}, u32[]{:S(2)}) async-start(bf16[8,4,1024]{2,1,0:T(4,128)(2,1)} %broadcast_in_dim.147), calls=%async_computation.8 | async-start | bytes 131072 | tf_op jit(solution)/shard_map/all_to_all | solution.py:16
  242.7 4.1 %all-to-all-done.8 = bf16[8,4,1024]{2,1,0:T(4,128)(2,1)S(1)} async-done(((bf16[8,4,1024]{2,1,0:T(4,128)(2,1)}), bf16[8,4,1024]{2,1,0:T(4,128)(2,1)S(1)}, u32[]{:S(2)}, u32[]{:S(2)}) %all-to-all-start.8) | async-done | bytes 65568 | tf_op jit(solution)/shard_map/all_to_all | solution.py:16
  248.3 3.8 %all-to-all-start = ((bf16[4,1024,256]{2,1,0:T(8,128)(2,1)}), bf16[4,1024,256]{2,1,0:T(8,128)(2,1)S(1)}, u32[]{:S(2)}, u32[]{:S(2)}) async-start(bf16[4,1024,256]{2,1,0:T(8,128)(2,1)} %broadcast_in_dim.142), calls=%async_computation | async-start | bytes 4194304 | tf_op jit(solution)/shard_map/all_to_all | solution.py:16
  255.8 43.8 %all-to-all-done = bf16[4,1024,256]{2,1,0:T(8,128)(2,1)S(1)} async-done(((bf16[4,1024,256]{2,1,0:T(8,128)(2,1)}), bf16[4,1024,256]{2,1,0:T(8,128)(2,1)S(1)}, u32[]{:S(2)}, u32[]{:S(2)}) %all-to-all-start) | async-done | bytes 2097184 | tf_op jit(solution)/shard_map/all_to_all | solution.py:16
  316.4 29.6 %all_to_all.57 = bf16[4,512,256]{2,1,0:T(8,128)(2,1)S(1)} all-to-all(bf16[4,512,256]{2,1,0:T(8,128)(2,1)S(1)} %broadcast_in_dim.169), channel_id=1, replica_groups=mesh['dp'=8,'tensor'=4] {'tensor'}, dimensions={0} | all-to-all | bytes 2097152 | tf_op jit(solution)/shard_map/all_to_all | solution.py:16
  346.6 4.3 %collective-permute-start.2 = (bf16[256,256]{1,0:T(8,128)(2,1)S(1)}, bf16[256,256]{1,0:T(8,128)(2,1)S(1)}, u32[]{:S(2)}, u32[]{:S(2)}) collective-permute-start(bf16[256,256]{1,0:T(8,128)(2,1)S(1)} %get-tuple-element.23), channel_id=1, source_target_pairs={{0,4},{4,8},{8,12},{12,16},{16,20},{20,24},{24,28},{1,5},{5,9},{9,... | collective-permute-start | bytes 393224 | tf_op jit(solution)/shard_map/ppermute | solution.py:28
  353.3 3.9 %collective-permute-done.3 = bf16[256,256]{1,0:T(8,128)(2,1)S(1)} collective-permute-done((bf16[256,256]{1,0:T(8,128)(2,1)S(1)}, bf16[256,256]{1,0:T(8,128)(2,1)S(1)}, u32[]{:S(2)}, u32[]{:S(2)}) %collective-permute-start.3) | collective-permute-done | bytes 131104 | tf_op jit(solution)/shard_map/ppermute | solution.py:29
  (97 shorter events, 41.7 us)
Async XLA Ops:
  6.5 160.5 %copy-start = (bf16[2048,256]{1,0:T(8,128)(2,1)S(1)}, bf16[2048,256]{1,0:T(8,128)(2,1)}, u32[]{:S(2)}) copy-start(bf16[2048,256]{1,0:T(8,128)(2,1)} %param.18) | copy-start | bytes 3145732
  6.5 108.0 %all-gather.4.cloned.1.call-start = ((), (), s32[]{:S(2)}) async-start(), calls=%async_computation.11 | async-start | bytes 9437184 | tf_op jit(solution)/shard_map/all_gather | solution.py:44
  7.3 122.5 %all-gather.6.cloned.1.call-start = ((), (), s32[]{:S(2)}) async-start(), calls=%async_computation.12 | async-start | bytes 9437184 | tf_op jit(solution)/shard_map/all_gather | solution.py:49
  11.6 98.5 %all-to-all-start.2 = ((bf16[4,1024,512]{2,1,0:T(8,128)(2,1)}), bf16[4,1024,512]{2,1,0:T(8,128)(2,1)}, u32[]{:S(2)}, u32[]{:S(2)}) async-start(bf16[4,1024,512]{2,1,0:T(8,128)(2,1)} %broadcast_in_dim.144), calls=%async_computation.2 | async-start | bytes 8388608 | tf_op jit(solution)/shard_map/all_to_all | solution.py:16
  17.1 201.3 %all-gather.8.cloned.1.call-start = ((), (), s32[]{:S(2)}) async-start(), calls=%async_computation.13 | async-start | bytes 5242880 | tf_op jit(solution)/shard_map/all_gather | solution.py:95
  129.7 22.6 %copy-start.1 = (bf16[1024,512]{1,0:T(8,128)(2,1)S(1)}, bf16[1024,512]{1,0:T(8,128)(2,1)}, u32[]{:S(2)}) copy-start(bf16[1024,512]{1,0:T(8,128)(2,1)} %param.14) | copy-start | bytes 3145732
  129.7 22.9 %copy-start.2 = (bf16[512,1024]{1,0:T(8,128)(2,1)S(1)}, bf16[512,1024]{1,0:T(8,128)(2,1)}, u32[]{:S(2)}) copy-start(bf16[512,1024]{1,0:T(8,128)(2,1)} %param.19) | copy-start | bytes 3145732
  146.3 44.0 %copy-start.8 = (bf16[512,256]{1,0:T(8,128)(2,1)S(1)}, bf16[512,256]{1,0:T(8,128)(2,1)}, u32[]{:S(2)}) copy-start(bf16[512,256]{1,0:T(8,128)(2,1)} %param.22) | copy-start | bytes 786436
  147.2 12.3 %all-to-all-start.3 = ((bf16[8,16,2048]{2,1,0:T(8,128)(2,1)}), bf16[8,16,2048]{2,1,0:T(8,128)(2,1)}, u32[]{:S(2)}, u32[]{:S(2)}) async-start(bf16[8,16,2048]{2,1,0:T(8,128)(2,1)} %broadcast_in_dim.145), calls=%async_computation.3 | async-start | bytes 1048576 | tf_op jit(solution)/shard_map/all_to_all | solution.py:16
  152.3 72.4 %copy-start.15 = (s32[16]{0:T(128)S(1)}, s32[16]{0:T(128)}, u32[]{:S(2)}) copy-start(s32[16]{0:T(128)} %param.21) | copy-start | bytes 196
  152.3 72.4 %copy-start.16 = (s32[16,1]{0,1:T(1,128)S(1)}, s32[16,1]{0,1:T(1,128)}, u32[]{:S(2)}) copy-start(s32[16,1]{0,1:T(1,128)} %param.20) | copy-start | bytes 196
  160.3 13.9 %all-to-all-start.6 = ((f32[8,16,1024]{2,1,0:T(8,128)}), f32[8,16,1024]{2,1,0:T(8,128)}, u32[]{:S(2)}, u32[]{:S(2)}) async-start(f32[8,16,1024]{2,1,0:T(8,128)} %broadcast_in_dim.146), calls=%async_computation.6 | async-start | bytes 1048576 | tf_op jit(solution)/shard_map/all_to_all | solution.py:16
  186.8 33.6 %all-to-all-start.7 = ((f32[4,32,1024]{2,1,0:T(8,128)}), f32[4,32,1024]{2,1,0:T(8,128)S(1)}, u32[]{:S(2)}, u32[]{:S(2)}) async-start(f32[4,32,1024]{2,1,0:T(8,128)} %bitcast.14), calls=%async_computation.7 | async-start | bytes 1048576 | tf_op jit(solution)/shard_map/all_to_all | solution.py:16
  190.4 52.3 %collective-permute-start = (bf16[256,256]{1,0:T(8,128)(2,1)S(1)}, bf16[256,256]{1,0:T(8,128)(2,1)S(1)}, u32[]{:S(2)}, u32[]{:S(2)}) collective-permute-start(bf16[256,256]{1,0:T(8,128)(2,1)S(1)} %get-tuple-element.25), channel_id=1, source_target_pairs={{0,4},{4,8},{8,12},{12,16},{16,20},{20,24},{24,28},{1,5},{5,9},{9,... | collective-permute-start | bytes 393224 | tf_op jit(solution)/shard_map/ppermute | solution.py:28
  196.0 46.6 %collective-permute-start.1 = (bf16[256,256]{1,0:T(8,128)(2,1)S(1)}, bf16[256,256]{1,0:T(8,128)(2,1)S(1)}, u32[]{:S(2)}, u32[]{:S(2)}) collective-permute-start(bf16[256,256]{1,0:T(8,128)(2,1)S(1)} %get-tuple-element.26), channel_id=1, source_target_pairs={{4,0},{8,4},{12,8},{16,12},{20,16},{24,20},{28,24},{5,1},{9,5},{13... | collective-permute-start | bytes 393224 | tf_op jit(solution)/shard_map/ppermute | solution.py:29
  220.5 9.0 %all-to-all-start.5 = ((f32[8,4,1024]{2,1,0:T(4,128)}), f32[8,4,1024]{2,1,0:T(4,128)S(1)}, u32[]{:S(2)}, u32[]{:S(2)}) async-start(f32[8,4,1024]{2,1,0:T(4,128)} %fusion.23), calls=%async_computation.5 | async-start | bytes 262144 | tf_op jit(solution)/shard_map/all_to_all | solution.py:16
  224.8 27.3 %copy-start.10 = (s32[4,6]{1,0:T(4,128)S(1)}, s32[4,6]{1,0:T(4,128)}, u32[]{:S(2)}) copy-start(s32[4,6]{1,0:T(4,128)} %param.23) | copy-start | bytes 292
  224.9 27.4 %copy-start.11 = (s32[4,6]{1,0:T(4,128)S(1)}, s32[4,6]{1,0:T(4,128)}, u32[]{:S(2)}) copy-start(s32[4,6]{1,0:T(4,128)} %param.24) | copy-start | bytes 292
  230.0 8.0 %all-to-all-start.1 = ((s32[8,1,16]{2,1,0:T(1,128)}), s32[8,1,16]{2,1,0:T(1,128)S(1)}, u32[]{:S(2)}, u32[]{:S(2)}) async-start(s32[8,1,16]{2,1,0:T(1,128)} %broadcast_in_dim.143), calls=%async_computation.1 | async-start | bytes 8192 | tf_op jit(solution)/shard_map/all_to_all | solution.py:16
  238.7 8.1 %all-to-all-start.8 = ((bf16[8,4,1024]{2,1,0:T(4,128)(2,1)}), bf16[8,4,1024]{2,1,0:T(4,128)(2,1)S(1)}, u32[]{:S(2)}, u32[]{:S(2)}) async-start(bf16[8,4,1024]{2,1,0:T(4,128)(2,1)} %broadcast_in_dim.147), calls=%async_computation.8 | async-start | bytes 131072 | tf_op jit(solution)/shard_map/all_to_all | solution.py:16
  248.3 51.3 %all-to-all-start = ((bf16[4,1024,256]{2,1,0:T(8,128)(2,1)}), bf16[4,1024,256]{2,1,0:T(8,128)(2,1)S(1)}, u32[]{:S(2)}, u32[]{:S(2)}) async-start(bf16[4,1024,256]{2,1,0:T(8,128)(2,1)} %broadcast_in_dim.142), calls=%async_computation | async-start | bytes 4194304 | tf_op jit(solution)/shard_map/all_to_all | solution.py:16
  300.3 9.1 %all-to-all-start.9 = ((bf16[4,32,1024]{2,1,0:T(8,128)(2,1)}), bf16[4,32,1024]{2,1,0:T(8,128)(2,1)S(1)}, u32[]{:S(2)}, u32[]{:S(2)}) async-start(bf16[4,32,1024]{2,1,0:T(8,128)(2,1)} %broadcast_in_dim.149), calls=%async_computation.9 | async-start | bytes 524288 | tf_op jit(solution)/shard_map/all_to_all | solution.py:16
  346.6 6.7 %collective-permute-start.2 = (bf16[256,256]{1,0:T(8,128)(2,1)S(1)}, bf16[256,256]{1,0:T(8,128)(2,1)S(1)}, u32[]{:S(2)}, u32[]{:S(2)}) collective-permute-start(bf16[256,256]{1,0:T(8,128)(2,1)S(1)} %get-tuple-element.23), channel_id=1, source_target_pairs={{0,4},{4,8},{8,12},{12,16},{16,20},{20,24},{24,28},{1,5},{5,9},{9,... | collective-permute-start | bytes 393224 | tf_op jit(solution)/shard_map/ppermute | solution.py:28
  350.9 6.3 %collective-permute-start.3 = (bf16[256,256]{1,0:T(8,128)(2,1)S(1)}, bf16[256,256]{1,0:T(8,128)(2,1)S(1)}, u32[]{:S(2)}, u32[]{:S(2)}) collective-permute-start(bf16[256,256]{1,0:T(8,128)(2,1)S(1)} %get-tuple-element.24), channel_id=1, source_target_pairs={{4,0},{8,4},{12,8},{16,12},{20,16},{24,20},{28,24},{5,1},{9,5},{13... | collective-permute-start | bytes 393224 | tf_op jit(solution)/shard_map/ppermute | solution.py:29
  (10 other events, 31.6 us)
Sparse Core Ops, SparseCore 0:
  9.2 56.8 all-gather.3
  68.1 54.3 all-gather.5
  124.1 94.3 all-gather.7

commit v2 on v1

--- a/solution.py
+++ b/solution.py
@@ -1,6 +1,10 @@
+import functools
+
 import jax
 import jax.numpy as jnp
 from jax import lax
+from jax.experimental import pallas as pl
+from jax.experimental.pallas import tpu as pltpu
 from jax.sharding import PartitionSpec as P
 
 TILE = 128
@@ -10,6 +14,7 @@
 eps = 1e-05
 f32 = jnp.float32
 bf16 = jnp.bfloat16
+MESH = pl.DeviceIdType.MESH
 
 
 def exchange(block, axis):
@@ -34,23 +39,308 @@
     return jnp.concatenate([blocks[i] for i in range(blocks.shape[0])], axis=1)
 
 
+def flip(index, bit):
+    return index + bit * (1 - 2 * ((index // bit) % 2))
+
+
+def owner_of(index, mask):
+    bit = 1
+    while bit <= mask:
+        if mask & bit:
+            index = flip(index, bit)
+        bit *= 2
+    return index
+
+
+def hop_plan(blocks, hops):
+    sent, order, turn = {}, [], 0
+    while len(sent) < blocks * hops:
+        pick = None
+        for block in range(blocks):
+            for hop in range(hops):
+                if (block, hop) in sent or pick is not None:
+                    continue
+                if hop == 0 or sent.get((block, hop - 1), turn) <= turn - 2:
+                    pick = (block, hop)
+        if pick is not None:
+            sent[pick] = turn
+        order.append(pick)
+        turn += 1
+    return order
+
+
+def cube_plan(bits, chunks):
+    came = {(array, 0, chunk): -2 for array in range(2) for chunk in range(chunks)}
+    wanted = {bit: [] for bit in bits}
+    for array in range(2):
+        span = [0]
+        for bit in bits if array == 0 else bits[::-1]:
+            for chunk in range(chunks):
+                wanted[bit] += [(chunk, len(span), array, mask) for mask in span]
+            span = span + [mask ^ bit for mask in span]
+    plan = {bit: [] for bit in bits}
+    turn = 0
+    while any(wanted.values()):
+        arrived = []
+        for bit in bits:
+            ready = [
+                item
+                for item in sorted(wanted[bit])
+                if came.get((item[2], item[3], item[0]), turn) <= turn - 2
+            ]
+            if ready:
+                chunk, _, array, mask = ready[0]
+                wanted[bit].remove(ready[0])
+                plan[bit].append((array, mask, chunk))
+                arrived.append((array, mask ^ bit, chunk))
+            else:
+                plan[bit].append(None)
+        for item in arrived:
+            came[item] = turn
+        turn += 1
+    return plan
+
+
+def front_kernel(
+    groups, parts, chunks, blocks, length, bits, hops, cube,
+    tok, gain, gw, uw, out, whole, normed, gfull, ufull,
+    hop_send, hop_recv, cube_send, cube_recv, pair_send, pair_recv, own_sem,
+):
+    me, col = lax.axis_index("dp"), lax.axis_index("tensor")
+    depth, width = gw.shape[0], gfull.shape[2]
+    rows, local = tok.shape[0] // blocks, tok.shape[1]
+    feed, full = (gw, uw), (gfull, ufull)
+
+    barrier = pltpu.get_barrier_semaphore()
+    partners = [flip(me, bit) for bit in [1] + bits]
+    for partner in partners:
+        pl.semaphore_signal(barrier, inc=1, device_id=(partner, col), device_id_type=MESH)
+
+    @pl.when(col > 0)
+    def _():
+        pl.semaphore_signal(barrier, inc=1, device_id=(me, col - 1), device_id_type=MESH)
+
+    @pl.when(col < parts - 1)
+    def _():
+        pl.semaphore_signal(barrier, inc=1, device_id=(me, col + 1), device_id_type=MESH)
+
+    own = [pltpu.make_async_copy(tok, whole.at[col], own_sem.at[0])]
+    for array in range(2):
+        for chunk in range(chunks):
+            own.append(
+                pltpu.make_async_copy(
+                    feed[array].at[:, pl.ds(chunk * width, width)],
+                    full[array].at[chunk, pl.ds(pl.multiple_of(me * depth, depth), depth)],
+                    own_sem.at[1 + array * chunks + chunk],
+                )
+            )
+    for copy in own:
+        copy.start()
+
+    sides = (col + parts - 1) // parts + (2 * parts - 2 - col) // parts
+    pl.semaphore_wait(barrier, len(partners) + sides)
+
+    def shard(array, mask, chunk):
+        at = pl.multiple_of(owner_of(me, mask) * depth, depth)
+        return full[array].at[chunk, pl.ds(at, depth)]
+
+    def swap(array, mask, chunk, bit, send, recv):
+        src = shard(array, mask, chunk)
+        if mask == 0:
+            src = feed[array].at[:, pl.ds(chunk * width, width)]
+        return pltpu.make_async_remote_copy(
+            src_ref=src,
+            dst_ref=shard(array, mask, chunk),
+            send_sem=send,
+            recv_sem=recv,
+            device_id=(flip(me, bit), col),
+            device_id_type=MESH,
+        )
+
+    def landed(array, mask, chunk, bit, send, recv):
+        there = shard(array, mask ^ bit, chunk)
+        return pltpu.make_async_remote_copy(
+            src_ref=there,
+            dst_ref=there,
+            send_sem=send,
+            recv_sem=recv,
+            device_id=(flip(me, bit), col),
+            device_id_type=MESH,
+        )
+
+    def hop(turn, way, incoming):
+        block, far = hops[turn]
+        step = 1 if way == 0 else -1
+        held = col - step * far
+        if incoming:
+            held = col - step * (far + 1)
+            there = (held >= 0) & (held < parts)
+        else:
+            there = (held >= 0) & (held < parts) & (col + step >= 0) & (col + step < parts)
+        span = pl.ds(block * rows, rows)
+        src = whole.at[held, span]
+        if not incoming and far == 0:
+            src = tok.at[span]
+        copy = pltpu.make_async_remote_copy(
+            src_ref=src,
+            dst_ref=whole.at[held, span],
+            send_sem=hop_send.at[way, turn],
+            recv_sem=hop_recv.at[way, turn],
+            device_id=(me, col + step),
+            device_id_type=MESH,
+        )
+        return there, copy
+
+    def pair(array, mask, chunk):
+        at = (array * (groups // 2) + mask // 2) * chunks + chunk
+        return array, mask, chunk, 1, pair_send.at[at], pair_recv.at[at]
+
+    def normalise(block):
+        def one(part, _):
+            span = pl.ds(pl.multiple_of(block * rows + part * length, length), length)
+            square = jnp.zeros((length, 1), f32)
+            for p in range(parts):
+                wide = whole[p, span, :].astype(f32)
+                square += jnp.sum(wide * wide, axis=1, keepdims=True)
+            scale = lax.rsqrt(square * (1.0 / (parts * local)) + eps)
+            for p in range(parts):
+                wide = whole[p, span, :].astype(f32)
+                normed[span, p * local : (p + 1) * local] = (
+                    wide * scale * gain[:, p * local : (p + 1) * local].astype(f32)
+                ).astype(bf16)
+            return 0
+
+        lax.fori_loop(0, rows // length, one, 0)
+
+    def work(block, chunk):
+        x = normed[pl.ds(pl.multiple_of(block * rows, rows), rows), :]
+        gate = jnp.dot(x, gfull[chunk], preferred_element_type=f32)
+        upward = jnp.dot(x, ufull[chunk], preferred_element_type=f32)
+        hidden = (gate / (1.0 + jnp.exp(-gate)) * upward).astype(bf16).astype(f32)
+        mean = jnp.sum(hidden.reshape(rows // length, length, width), axis=1)
+        out[chunk, block] = mean * (1.0 / length)
+
+    turns = max([len(hops)] + [len(cube[bit]) for bit in bits])
+    missing = {chunk: 2 * groups for chunk in range(chunks)}
+    unhopped = {block: parts - 1 for block in range(blocks)}
+    ready_chunks, ready_blocks = [], []
+    flying = []
+
+    for array in range(2):
+        for chunk in range(chunks):
+            swap(*pair(array, 0, chunk)).start()
+            flying.append((array, 0, chunk))
+    for turn in range(turns + 3):
+        back = turn - 2
+        new_blocks, new_chunks = [], []
+        settled = flying
+        flying = []
+        if 0 <= back < turns:
+            if back < len(hops) and hops[back] is not None:
+                for way in range(2):
+                    there, copy = hop(back, way, True)
+                    pl.when(there)(copy.wait_recv)
+                    there, copy = hop(back, way, False)
+                    pl.when(there)(copy.wait_send)
+                unhopped[hops[back][0]] -= 1
+                if unhopped[hops[back][0]] == 0:
+                    new_blocks.append(hops[back][0])
+            for n, bit in enumerate(bits):
+                item = cube[bit][back] if back < len(cube[bit]) else None
+                if item is not None:
+                    sems = (cube_send.at[n, back], cube_recv.at[n, back])
+                    landed(*item, bit, *sems).wait_recv()
+                    swap(*item, bit, *sems).wait_send()
+                    moved = (item[0], item[1] ^ bit, item[2])
+                    swap(*pair(*moved)).start()
+                    flying.append(moved)
+        if turn < len(hops) and hops[turn] is not None:
+            for way in range(2):
+                there, copy = hop(turn, way, False)
+                pl.when(there)(copy.start)
+        for n, bit in enumerate(bits):
+            item = cube[bit][turn] if turn < len(cube[bit]) else None
+            if item is not None:
+                swap(*item, bit, cube_send.at[n, turn], cube_recv.at[n, turn]).start()
+        if turn == 0:
+            for copy in own:
+                copy.wait()
+            for chunk in range(chunks):
+                missing[chunk] -= 2
+        for block in new_blocks:
+            normalise(block)
+            if ready_chunks:
+                def across(n, _, block=block):
+                    work(block, n)
+                    return 0
+                lax.fori_loop(0, len(ready_chunks), across, 0)
+            ready_blocks.append(block)
+        for array, mask, chunk in settled:
+            landed(*pair(array, mask, chunk)).wait_recv()
+            swap(*pair(array, mask, chunk)).wait_send()
+            missing[chunk] -= 1
+        for array, mask, chunk in settled:
+            if mask:
+                missing[chunk] -= 1
+        for chunk in range(chunks):
+            if missing[chunk] == 0 and chunk not in ready_chunks:
+                assert chunk == len(ready_chunks)
+                if ready_blocks:
+                    assert ready_blocks == list(range(len(ready_blocks)))
+                    def down(n, _, chunk=chunk):
+                        work(n, chunk)
+                        return 0
+                    lax.fori_loop(0, len(ready_blocks), down, 0)
+                ready_chunks.append(chunk)
+    assert len(ready_chunks) == chunks and len(ready_blocks) == blocks and not flying
+
+
 def pooled_hidden(token_states, norm_gain, gate_weight, up_weight, length):
-    whole = side_by_side(spread(token_states, "tensor"))
-    wide = whole.astype(f32)
-    square = jnp.mean(wide * wide, axis=1, keepdims=True)
-    normed = (wide * lax.rsqrt(square + eps) * norm_gain.astype(f32)).astype(bf16)
-    gate = jnp.dot(
-        normed,
-        lax.all_gather(gate_weight, "dp", axis=0, tiled=True),
-        preferred_element_type=f32,
-    )
-    upward = jnp.dot(
-        normed,
-        lax.all_gather(up_weight, "dp", axis=0, tiled=True),
-        preferred_element_type=f32,
-    )
-    hidden = (jax.nn.silu(gate) * upward).astype(bf16)
-    return jnp.mean(hidden.astype(f32).reshape(-1, length, hidden.shape[1]), axis=1)
+    groups, parts = lax.axis_size("dp"), lax.axis_size("tensor")
+    tokens, local = token_states.shape
+    depth, hidden = gate_weight.shape
+    chunks = blocks = 4
+    width, rows = hidden // chunks, tokens // blocks
+    bits = [1 << n for n in range(1, (groups - 1).bit_length())]
+    hops = hop_plan(blocks, parts - 1)
+    cube = cube_plan(bits, chunks)
+    turns = max(len(cube[bit]) for bit in bits)
+    pairs = 2 * chunks * (groups // 2)
+    sem = pltpu.SemaphoreType.DMA
+    features = parts * local
+    any_space = pl.BlockSpec(memory_space=pl.ANY)
+    vmem = pl.BlockSpec(memory_space=pltpu.VMEM)
+    mean = pl.pallas_call(
+        functools.partial(
+            front_kernel, groups, parts, chunks, blocks, length, bits, hops, cube
+        ),
+        out_shape=jax.ShapeDtypeStruct((chunks, blocks, rows // length, width), f32),
+        in_specs=[any_space, vmem, any_space, any_space],
+        out_specs=vmem,
+        scratch_shapes=[
+            pltpu.VMEM((parts, tokens, local), bf16),
+            pltpu.VMEM((tokens, features), bf16),
+            pltpu.VMEM((chunks, groups * depth, width), bf16),
+            pltpu.VMEM((chunks, groups * depth, width), bf16),
+            sem((2, len(hops))),
+            sem((2, len(hops))),
+            sem((len(bits), turns)),
+            sem((len(bits), turns)),
+            sem((pairs,)),
+            sem((pairs,)),
+            sem((1 + 2 * chunks,)),
+        ],
+        compiler_params=pltpu.CompilerParams(
+            collective_id=0, has_side_effects=True, vmem_limit_bytes=48 << 20
+        ),
+        cost_estimate=pl.CostEstimate(
+            flops=4 * tokens * features * hidden,
+            bytes_accessed=4 * features * hidden,
+            transcendentals=tokens * hidden,
+        ),
+        name="gather_and_pool",
+    )(token_states, norm_gain[None], gate_weight, up_weight)
+    return jnp.transpose(mean, (1, 2, 0, 3)).reshape(tokens // length, hidden)
 
 
 def per_device(

time: 366 us -> 361 us (0.986)
  Pallas kernels: 0 us -> 150 us
  waiting for transfers between devices: 190 us -> 73.6 us
  matrix products: 43.6 us -> 11.8 us
  blocking collectives: 42.2 us -> 37.7 us
    pallas_call x0 -> x1, Pallas kernels: none -> 150 us  [pooled_hidden(): pl.pallas_call(functools.partial(front_kernel, groups, parts, chunks, blo...]
    all_to_all x9 -> x8, waiting for transfers between devices: 164 us -> 71.3 us  [exchange(): return lax.all_to_all(block, axis, split_axis=0, concat_axis=0, tiled=True)]
    dot_general x2 -> x0, matrix products: 31.7 us -> none  [the longest x1 16.6 us: pooled_hidden(): jnp.dot(normed, lax.all_gather(up_weight, 'dp', axis=0, tiled=True), pref...]
    all_gather x1, waiting for transfers between devices: 20.4 us -> 0.02 us  [per_device(): whole_embed = lax.all_gather(embed_weight, 'tensor', axis=0, tiled=True)]
    ppermute x2, starting transfers between devices: 3.84 us -> 10.2 us  [with_halo(): high = lax.ppermute(block[:width], 'dp', backward)]
    ppermute x2, starting transfers between devices: 9.98 us -> 4.73 us  [with_halo(): low = lax.ppermute(block[block.shape[0] - width:], 'dp', forward)]
    all_to_all x2, blocking collectives: 42.2 us -> 37.7 us  [exchange(): return lax.all_to_all(block, axis, split_axis=0, concat_axis=0, tiled=True)]
    broadcast_in_dim x9 -> x8, local copies, waits for them, and re-layouts: 8.81 us -> 5.27 us  [spread(): return exchange(jnp.broadcast_to(block[None], (count,) + block.shape), axis)]
  transfers between devices with their start and end apart: 16 -> 13, of which waited for: 10 -> 9; matrix products, arithmetic and copies ran while one was open for 14% -> 4% of each run, Pallas kernels for 0% -> 42%
where the time goes in v2:
time: 361 us; the launch traced here: 360 us
  Pallas kernels  150 us (42%)
  waiting for transfers between devices  73.6 us (20%)
  starting transfers between devices  55.1 us (15%)
  blocking collectives  37.7 us (10%)
  between operations  13.8 us (4%)
  local copies, waits for them, and re-layouts  13.7 us (4%)
  matrix products  11.8 us (3%)
  other arithmetic  4.36 us (1%)
    pallas_call x1, Pallas kernels, pooled_hidden(): pl.pallas_call(functools.partial(front_kernel, groups, parts, chunks, blo...  150 us
    all_to_all x8, waiting for transfers between devices, exchange(): return lax.all_to_all(block, axis, split_axis=0, concat_axis=0, tiled=True)  71.3 us
    all_to_all x8, starting transfers between devices, exchange(): return lax.all_to_all(block, axis, split_axis=0, concat_axis=0, tiled=True)  40.2 us
    all_to_all x2, blocking collectives, exchange(): return lax.all_to_all(block, axis, split_axis=0, concat_axis=0, tiled=True)  37.7 us
    ppermute x2, starting transfers between devices, with_halo(): high = lax.ppermute(block[:width], 'dp', backward)  10.2 us
  transfers between devices with their start and end apart: 13, of which 9 were waited for; matrix products, arithmetic and copies ran while one was open for 4% of the time, Pallas kernels for 42%

profile of v2, /device:TPU:1, one launch (start us, length us, event | category | flops | bytes accessed | tf_op | source)
XLA Modules:
  0.0 359.6 jit_solution(541172894844618741)
XLA Ops:
  11.6 149.7 %gather_and_pool.1 = f32[4,4,4,512]{3,2,1,0:T(4,128)S(1)} custom-call(bf16[1024,512]{1,0:T(8,128)(2,1)S(1)} %copy-done.1, bf16[1,2048]{1,0:T(2,128)(2,1)S(1)} %broadcast_in_dim.139.gain, bf16[256,2048]{1,0:T(8,128)(2,1)S(1)} %copy-done.3, bf16[256,2048]{1,0:T(8,128)(2,1)S(1)} %copy-done.4), custom_call_target="tpu_custom_call" | custom-call | flops 17179869184 | bytes 16777216 | tf_op jit(solution)/shard_map/gather_and_pool/pallas_call | solution.py:313
  162.3 5.3 %all-to-all-start.2 = ((bf16[8,16,2048]{2,1,0:T(8,128)(2,1)}), bf16[8,16,2048]{2,1,0:T(8,128)(2,1)}, u32[]{:S(2)}, u32[]{:S(2)}) async-start(bf16[8,16,2048]{2,1,0:T(8,128)(2,1)} %broadcast_in_dim.140), calls=%async_computation.2 | async-start | bytes 1048576 | tf_op jit(solution)/shard_map/all_to_all | solution.py:21
  168.4 6.1 %all-to-all-done.2 = bf16[8,16,2048]{2,1,0:T(8,128)(2,1)} async-done(((bf16[8,16,2048]{2,1,0:T(8,128)(2,1)}), bf16[8,16,2048]{2,1,0:T(8,128)(2,1)}, u32[]{:S(2)}, u32[]{:S(2)}) %all-to-all-start.2) | async-done | bytes 524320 | tf_op jit(solution)/shard_map/all_to_all | solution.py:21
  175.4 7.2 %all-to-all-start.5 = ((f32[8,16,1024]{2,1,0:T(8,128)}), f32[8,16,1024]{2,1,0:T(8,128)}, u32[]{:S(2)}, u32[]{:S(2)}) async-start(f32[8,16,1024]{2,1,0:T(8,128)} %broadcast_in_dim.141), calls=%async_computation.5 | async-start | bytes 1048576 | tf_op jit(solution)/shard_map/all_to_all | solution.py:21
  183.9 5.5 %all-to-all-done.5 = f32[8,16,1024]{2,1,0:T(8,128)} async-done(((f32[8,16,1024]{2,1,0:T(8,128)}), f32[8,16,1024]{2,1,0:T(8,128)}, u32[]{:S(2)}, u32[]{:S(2)}) %all-to-all-start.5) | async-done | bytes 524320 | tf_op jit(solution)/shard_map/all_to_all | solution.py:21
  189.4 8.0 %all_to_all.51 = f32[4,32,256]{2,1,0:T(8,128)S(1)} all-to-all(f32[4,32,256]{2,1,0:T(8,128)S(1)} %fusion.8), channel_id=1, replica_groups=mesh['dp'=8,'tensor'=4] {'tensor'}, dimensions={0} | all-to-all | bytes 262144 | tf_op jit(solution)/shard_map/all_to_all | solution.py:21
  197.4 3.5 all-to-all-start.6
  200.9 6.4 %collective-permute-start.1 = (bf16[256,256]{1,0:T(8,128)(2,1)S(1)}, bf16[256,256]{1,0:T(8,128)(2,1)S(1)}, u32[]{:S(2)}, u32[]{:S(2)}) collective-permute-start(bf16[256,256]{1,0:T(8,128)(2,1)S(1)} %get-tuple-element.22), channel_id=1, source_target_pairs={{4,0},{8,4},{12,8},{16,12},{20,16},{24,20},{28,24},{5,1},{9,5},{13... | collective-permute-start | bytes 393224 | tf_op jit(solution)/shard_map/ppermute | solution.py:34
  207.3 2.3 collective-permute-start
  211.8 9.1 %all-to-all-start.4 = ((f32[8,4,1024]{2,1,0:T(4,128)}), f32[8,4,1024]{2,1,0:T(4,128)S(1)}, u32[]{:S(2)}, u32[]{:S(2)}) async-start(f32[8,4,1024]{2,1,0:T(4,128)} %fusion.17), calls=%async_computation.4 | async-start | bytes 262144 | tf_op jit(solution)/shard_map/all_to_all | solution.py:21
  220.9 4.6 %all-to-all-done.4 = f32[8,4,1024]{2,1,0:T(4,128)S(1)} async-done(((f32[8,4,1024]{2,1,0:T(4,128)}), f32[8,4,1024]{2,1,0:T(4,128)S(1)}, u32[]{:S(2)}, u32[]{:S(2)}) %all-to-all-start.4) | async-done | bytes 131104 | tf_op jit(solution)/shard_map/all_to_all | solution.py:21
  226.1 4.1 %all-to-all-start.1 = ((s32[8,1,16]{2,1,0:T(1,128)}), s32[8,1,16]{2,1,0:T(1,128)S(1)}, u32[]{:S(2)}, u32[]{:S(2)}) async-start(s32[8,1,16]{2,1,0:T(1,128)} %broadcast_in_dim.138), calls=%async_computation.1 | async-start | bytes 8192 | tf_op jit(solution)/shard_map/all_to_all | solution.py:21
  230.2 3.9 %all-to-all-done.1 = s32[8,1,16]{2,1,0:T(1,128)S(1)} async-done(((s32[8,1,16]{2,1,0:T(1,128)}), s32[8,1,16]{2,1,0:T(1,128)S(1)}, u32[]{:S(2)}, u32[]{:S(2)}) %all-to-all-start.1) | async-done | bytes 544 | tf_op jit(solution)/shard_map/all_to_all | solution.py:21
  234.8 4.0 %all-to-all-start.7 = ((bf16[8,4,1024]{2,1,0:T(4,128)(2,1)}), bf16[8,4,1024]{2,1,0:T(4,128)(2,1)S(1)}, u32[]{:S(2)}, u32[]{:S(2)}) async-start(bf16[8,4,1024]{2,1,0:T(4,128)(2,1)} %broadcast_in_dim.142), calls=%async_computation.7 | async-start | bytes 131072 | tf_op jit(solution)/shard_map/all_to_all | solution.py:21
  238.8 4.1 %all-to-all-done.7 = bf16[8,4,1024]{2,1,0:T(4,128)(2,1)S(1)} async-done(((bf16[8,4,1024]{2,1,0:T(4,128)(2,1)}), bf16[8,4,1024]{2,1,0:T(4,128)(2,1)S(1)}, u32[]{:S(2)}, u32[]{:S(2)}) %all-to-all-start.7) | async-done | bytes 65568 | tf_op jit(solution)/shard_map/all_to_all | solution.py:21
  244.4 3.7 %all-to-all-start = ((bf16[4,1024,256]{2,1,0:T(8,128)(2,1)}), bf16[4,1024,256]{2,1,0:T(8,128)(2,1)S(1)}, u32[]{:S(2)}, u32[]{:S(2)}) async-start(bf16[4,1024,256]{2,1,0:T(8,128)(2,1)} %broadcast_in_dim.137), calls=%async_computation | async-start | bytes 4194304 | tf_op jit(solution)/shard_map/all_to_all | solution.py:21
  251.8 44.0 %all-to-all-done = bf16[4,1024,256]{2,1,0:T(8,128)(2,1)S(1)} async-done(((bf16[4,1024,256]{2,1,0:T(8,128)(2,1)}), bf16[4,1024,256]{2,1,0:T(8,128)(2,1)S(1)}, u32[]{:S(2)}, u32[]{:S(2)}) %all-to-all-start) | async-done | bytes 2097184 | tf_op jit(solution)/shard_map/all_to_all | solution.py:21
  296.5 3.4 all-to-all-start.8
  302.6 3.1 all-to-all-done.8
  305.7 2.4 add_convert_fusion
  310.2 3.0 fusion.3
  313.3 29.6 %all_to_all.52 = bf16[4,512,256]{2,1,0:T(8,128)(2,1)S(1)} all-to-all(bf16[4,512,256]{2,1,0:T(8,128)(2,1)S(1)} %broadcast_in_dim.164), channel_id=1, replica_groups=mesh['dp'=8,'tensor'=4] {'tensor'}, dimensions={0} | all-to-all | bytes 2097152 | tf_op jit(solution)/shard_map/all_to_all | solution.py:21
  343.5 3.8 %collective-permute-start.3 = (bf16[256,256]{1,0:T(8,128)(2,1)S(1)}, bf16[256,256]{1,0:T(8,128)(2,1)S(1)}, u32[]{:S(2)}, u32[]{:S(2)}) collective-permute-start(bf16[256,256]{1,0:T(8,128)(2,1)S(1)} %get-tuple-element.20), channel_id=1, source_target_pairs={{4,0},{8,4},{12,8},{16,12},{20,16},{24,20},{28,24},{5,1},{9,5},{13... | collective-permute-start | bytes 393224 | tf_op jit(solution)/shard_map/ppermute | solution.py:34
  347.3 2.4 collective-permute-start.2
  (82 shorter events, 26.7 us)
Async XLA Ops:
  6.5 176.0 %copy-start = (bf16[2048,256]{1,0:T(8,128)(2,1)S(1)}, bf16[2048,256]{1,0:T(8,128)(2,1)}, u32[]{:S(2)}) copy-start(bf16[2048,256]{1,0:T(8,128)(2,1)} %param.18) | copy-start | bytes 3145732
  6.5 203.1 %all-gather.2.cloned.1.call-start = ((), (), s32[]{:S(2)}) async-start(), calls=%async_computation.10 | async-start | bytes 5242880 | tf_op jit(solution)/shard_map/all_gather | solution.py:385
  161.3 6.3 %copy-start.2 = (bf16[1024,512]{1,0:T(8,128)(2,1)S(1)}, bf16[1024,512]{1,0:T(8,128)(2,1)}, u32[]{:S(2)}) copy-start(bf16[1024,512]{1,0:T(8,128)(2,1)} %tok.1) | copy-start | bytes 3145732
  161.3 6.5 %copy-start.5 = (bf16[512,1024]{1,0:T(8,128)(2,1)S(1)}, bf16[512,1024]{1,0:T(8,128)(2,1)}, u32[]{:S(2)}) copy-start(bf16[512,1024]{1,0:T(8,128)(2,1)} %param.19) | copy-start | bytes 3145732
  162.3 12.2 %all-to-all-start.2 = ((bf16[8,16,2048]{2,1,0:T(8,128)(2,1)}), bf16[8,16,2048]{2,1,0:T(8,128)(2,1)}, u32[]{:S(2)}, u32[]{:S(2)}) async-start(bf16[8,16,2048]{2,1,0:T(8,128)(2,1)} %broadcast_in_dim.140), calls=%async_computation.2 | async-start | bytes 1048576 | tf_op jit(solution)/shard_map/all_to_all | solution.py:21
  175.4 25.5 %copy-start.7 = (bf16[512,256]{1,0:T(8,128)(2,1)S(1)}, bf16[512,256]{1,0:T(8,128)(2,1)}, u32[]{:S(2)}) copy-start(bf16[512,256]{1,0:T(8,128)(2,1)} %param.22) | copy-start | bytes 786436
  175.4 14.0 %all-to-all-start.5 = ((f32[8,16,1024]{2,1,0:T(8,128)}), f32[8,16,1024]{2,1,0:T(8,128)}, u32[]{:S(2)}, u32[]{:S(2)}) async-start(f32[8,16,1024]{2,1,0:T(8,128)} %broadcast_in_dim.141), calls=%async_computation.5 | async-start | bytes 1048576 | tf_op jit(solution)/shard_map/all_to_all | solution.py:21
  182.5 38.3 %copy-start.13 = (s32[16]{0:T(128)S(1)}, s32[16]{0:T(128)}, u32[]{:S(2)}) copy-start(s32[16]{0:T(128)} %param.21) | copy-start | bytes 196
  182.5 38.3 %copy-start.14 = (s32[16,1]{0,1:T(1,128)S(1)}, s32[16,1]{0,1:T(1,128)}, u32[]{:S(2)}) copy-start(s32[16,1]{0,1:T(1,128)} %param.20) | copy-start | bytes 196
  197.4 14.3 %all-to-all-start.6 = ((f32[4,32,1024]{2,1,0:T(8,128)}), f32[4,32,1024]{2,1,0:T(8,128)S(1)}, u32[]{:S(2)}, u32[]{:S(2)}) async-start(f32[4,32,1024]{2,1,0:T(8,128)} %bitcast.10), calls=%async_computation.6 | async-start | bytes 1048576 | tf_op jit(solution)/shard_map/all_to_all | solution.py:21
  200.9 37.8 %collective-permute-start.1 = (bf16[256,256]{1,0:T(8,128)(2,1)S(1)}, bf16[256,256]{1,0:T(8,128)(2,1)S(1)}, u32[]{:S(2)}, u32[]{:S(2)}) collective-permute-start(bf16[256,256]{1,0:T(8,128)(2,1)S(1)} %get-tuple-element.22), channel_id=1, source_target_pairs={{4,0},{8,4},{12,8},{16,12},{20,16},{24,20},{28,24},{5,1},{9,5},{13... | collective-permute-start | bytes 393224 | tf_op jit(solution)/shard_map/ppermute | solution.py:34
  207.3 31.4 %collective-permute-start = (bf16[256,256]{1,0:T(8,128)(2,1)S(1)}, bf16[256,256]{1,0:T(8,128)(2,1)S(1)}, u32[]{:S(2)}, u32[]{:S(2)}) collective-permute-start(bf16[256,256]{1,0:T(8,128)(2,1)S(1)} %get-tuple-element.21), channel_id=1, source_target_pairs={{0,4},{4,8},{8,12},{12,16},{16,20},{20,24},{24,28},{1,5},{5,9},{9,... | collective-permute-start | bytes 393224 | tf_op jit(solution)/shard_map/ppermute | solution.py:33
  211.8 13.7 %all-to-all-start.4 = ((f32[8,4,1024]{2,1,0:T(4,128)}), f32[8,4,1024]{2,1,0:T(4,128)S(1)}, u32[]{:S(2)}, u32[]{:S(2)}) async-start(f32[8,4,1024]{2,1,0:T(4,128)} %fusion.17), calls=%async_computation.4 | async-start | bytes 262144 | tf_op jit(solution)/shard_map/all_to_all | solution.py:21
  226.1 8.0 %all-to-all-start.1 = ((s32[8,1,16]{2,1,0:T(1,128)}), s32[8,1,16]{2,1,0:T(1,128)S(1)}, u32[]{:S(2)}, u32[]{:S(2)}) async-start(s32[8,1,16]{2,1,0:T(1,128)} %broadcast_in_dim.138), calls=%async_computation.1 | async-start | bytes 8192 | tf_op jit(solution)/shard_map/all_to_all | solution.py:21
  234.8 8.1 %all-to-all-start.7 = ((bf16[8,4,1024]{2,1,0:T(4,128)(2,1)}), bf16[8,4,1024]{2,1,0:T(4,128)(2,1)S(1)}, u32[]{:S(2)}, u32[]{:S(2)}) async-start(bf16[8,4,1024]{2,1,0:T(4,128)(2,1)} %broadcast_in_dim.142), calls=%async_computation.7 | async-start | bytes 131072 | tf_op jit(solution)/shard_map/all_to_all | solution.py:21
  244.4 3.8 %copy-start.8 = (s32[4,6]{1,0:T(4,128)S(1)}, s32[4,6]{1,0:T(4,128)}, u32[]{:S(2)}) copy-start(s32[4,6]{1,0:T(4,128)} %param.23) | copy-start | bytes 292
  244.4 3.9 %copy-start.9 = (s32[4,6]{1,0:T(4,128)S(1)}, s32[4,6]{1,0:T(4,128)}, u32[]{:S(2)}) copy-start(s32[4,6]{1,0:T(4,128)} %param.24) | copy-start | bytes 292
  244.4 51.4 %all-to-all-start = ((bf16[4,1024,256]{2,1,0:T(8,128)(2,1)}), bf16[4,1024,256]{2,1,0:T(8,128)(2,1)S(1)}, u32[]{:S(2)}, u32[]{:S(2)}) async-start(bf16[4,1024,256]{2,1,0:T(8,128)(2,1)} %broadcast_in_dim.137), calls=%async_computation | async-start | bytes 4194304 | tf_op jit(solution)/shard_map/all_to_all | solution.py:21
  296.5 9.1 %all-to-all-start.8 = ((bf16[4,32,1024]{2,1,0:T(8,128)(2,1)}), bf16[4,32,1024]{2,1,0:T(8,128)(2,1)S(1)}, u32[]{:S(2)}, u32[]{:S(2)}) async-start(bf16[4,32,1024]{2,1,0:T(8,128)(2,1)} %broadcast_in_dim.144), calls=%async_computation.8 | async-start | bytes 524288 | tf_op jit(solution)/shard_map/all_to_all | solution.py:21
  305.7 2.4 copy-start.11
  308.1 2.1 copy-start.10
  343.0 6.7 %copy-start.12 = (bf16[1024,256]{1,0:T(8,128)(2,1)S(1)}, bf16[1024,256]{1,0:T(8,128)(2,1)}, u32[]{:S(2)}) copy-start(bf16[1024,256]{1,0:T(8,128)(2,1)} %param.26) | copy-start | bytes 1572868
  343.5 7.0 %collective-permute-start.3 = (bf16[256,256]{1,0:T(8,128)(2,1)S(1)}, bf16[256,256]{1,0:T(8,128)(2,1)S(1)}, u32[]{:S(2)}, u32[]{:S(2)}) collective-permute-start(bf16[256,256]{1,0:T(8,128)(2,1)S(1)} %get-tuple-element.20), channel_id=1, source_target_pairs={{4,0},{8,4},{12,8},{16,12},{20,16},{24,20},{28,24},{5,1},{9,5},{13... | collective-permute-start | bytes 393224 | tf_op jit(solution)/shard_map/ppermute | solution.py:34
  347.3 4.4 %collective-permute-start.2 = (bf16[256,256]{1,0:T(8,128)(2,1)S(1)}, bf16[256,256]{1,0:T(8,128)(2,1)S(1)}, u32[]{:S(2)}, u32[]{:S(2)}) collective-permute-start(bf16[256,256]{1,0:T(8,128)(2,1)S(1)} %get-tuple-element.19), channel_id=1, source_target_pairs={{0,4},{4,8},{8,12},{12,16},{16,20},{20,24},{24,28},{1,5},{5,9},{9,... | collective-permute-start | bytes 393224 | tf_op jit(solution)/shard_map/ppermute | solution.py:33
  (5 other events, 7.0 us)
Sparse Core Ops, SparseCore 0:
  8.9 114.7 all-gather.1

commit v3 on v2

--- a/solution.py
+++ b/solution.py
@@ -15,28 +15,6 @@
 f32 = jnp.float32
 bf16 = jnp.bfloat16
 MESH = pl.DeviceIdType.MESH
-
-
-def exchange(block, axis):
-    return lax.all_to_all(block, axis, split_axis=0, concat_axis=0, tiled=True)
-
-
-def spread(block, axis):
-    count = lax.axis_size(axis)
-    return exchange(jnp.broadcast_to(block[None], (count,) + block.shape), axis)
-
-
-def with_halo(block, width):
-    count = lax.axis_size("dp")
-    forward = [(i, i + 1) for i in range(count - 1)]
-    backward = [(target, source) for source, target in forward]
-    low = lax.ppermute(block[block.shape[0] - width :], "dp", forward)
-    high = lax.ppermute(block[:width], "dp", backward)
-    return jnp.concatenate([low, block, high], axis=0)
-
-
-def side_by_side(blocks):
-    return jnp.concatenate([blocks[i] for i in range(blocks.shape[0])], axis=1)
 
 
 def flip(index, bit):
@@ -103,7 +81,7 @@
 
 def front_kernel(
     groups, parts, chunks, blocks, length, bits, hops, cube,
-    tok, gain, gw, uw, out, whole, normed, gfull, ufull,
+    tok, gain, gw, uw, out, own_mean, whole, normed, gfull, ufull,
     hop_send, hop_recv, cube_send, cube_recv, pair_send, pair_recv, own_sem,
 ):
     me, col = lax.axis_index("dp"), lax.axis_index("tensor")
@@ -265,6 +243,15 @@
         if turn == 0:
             for copy in own:
                 copy.wait()
+
+            def average(text, _):
+                span = pl.ds(pl.multiple_of(text * length, length), length)
+                own_mean[text] = jnp.sum(
+                    whole[col, span, :].astype(f32), axis=0, keepdims=True
+                ) * (1.0 / length)
+                return 0
+
+            lax.fori_loop(0, tok.shape[0] // length, average, 0)
             for chunk in range(chunks):
                 missing[chunk] -= 2
         for block in new_blocks:
@@ -310,13 +297,16 @@
     features = parts * local
     any_space = pl.BlockSpec(memory_space=pl.ANY)
     vmem = pl.BlockSpec(memory_space=pltpu.VMEM)
-    mean = pl.pallas_call(
+    mean, own_mean = pl.pallas_call(
         functools.partial(
             front_kernel, groups, parts, chunks, blocks, length, bits, hops, cube
         ),
-        out_shape=jax.ShapeDtypeStruct((chunks, blocks, rows // length, width), f32),
+        out_shape=[
+            jax.ShapeDtypeStruct((chunks, blocks, rows // length, width), f32),
+            jax.ShapeDtypeStruct((tokens // length, 1, local), f32),
+        ],
         in_specs=[any_space, vmem, any_space, any_space],
-        out_specs=vmem,
+        out_specs=[vmem, vmem],
         scratch_shapes=[
             pltpu.VMEM((parts, tokens, local), bf16),
             pltpu.VMEM((tokens, features), bf16),
@@ -340,7 +330,272 @@
         ),
         name="gather_and_pool",
     )(token_states, norm_gain[None], gate_weight, up_weight)
-    return jnp.transpose(mean, (1, 2, 0, 3)).reshape(tokens // length, hidden)
+    mean = jnp.transpose(mean, (1, 2, 0, 3)).reshape(tokens // length, hidden)
+    return mean, own_mean[:, 0]
+
+
+def line_copies(buffer, col, parts, me, cuts, send, recv):
+    size = buffer.shape[1] // cuts
+
+    def copy(way, far, cut, incoming):
+        step = 1 if way == 0 else -1
+        held = col - step * (far + 1 if incoming else far)
+        there = (held >= 0) & (held < parts)
+        if not incoming:
+            there = there & (col + step >= 0) & (col + step < parts)
+        part = buffer.at[held, pl.ds(cut * size, size)]
+        return there, pltpu.make_async_remote_copy(
+            src_ref=part,
+            dst_ref=part,
+            send_sem=send.at[way, far, cut],
+            recv_sem=recv.at[way, far, cut],
+            device_id=(me, col + step),
+            device_id_type=MESH,
+        )
+
+    def advance(far):
+        for cut in range(cuts):
+            for way in range(2):
+                if far > 0:
+                    there, came = copy(way, far - 1, cut, True)
+                    pl.when(there)(came.wait_recv)
+                if far < parts - 1:
+                    there, gone = copy(way, far, cut, False)
+                    pl.when(there)(gone.start)
+
+    def finish():
+        for far in range(parts - 1):
+            for cut in range(cuts):
+                for way in range(2):
+                    there, gone = copy(way, far, cut, False)
+                    pl.when(there)(gone.wait_send)
+
+    return advance, finish
+
+
+def tail_kernel(
+    groups, parts, layers, cuts,
+    mean, token_mean, down, embed, place, cache, adjacency, self_w, near_w, out,
+    hidden, spots, share, pooled, terms, sums, fresh, states, nodes, extended,
+    a_send, a_recv, p_send, p_recv, b_send, b_recv, c_send, c_recv,
+    d_send, d_recv, e_send, e_recv, line_send, line_recv, halo_send, halo_recv,
+):
+    me, col = lax.axis_index("dp"), lax.axis_index("tensor")
+    texts, width = mean.shape[0], down.shape[1]
+    count, local = cache.shape
+    halo = (extended.shape[1] - count) // 2
+    split = groups // parts
+
+    barrier = pltpu.get_barrier_semaphore()
+    for s in range(1, groups):
+        pl.semaphore_signal(
+            barrier, inc=1, device_id=((me + s) % groups, col), device_id_type=MESH
+        )
+    for s in range(1, parts):
+        pl.semaphore_signal(
+            barrier, inc=1, device_id=(me, (col + s) % parts), device_id_type=MESH
+        )
+    hidden[me] = mean[...].astype(bf16)
+    spots[me] = place[...]
+    nodes[0, col] = cache[...]
+    pl.semaphore_wait(barrier, groups + parts - 2)
+
+    def along(axis, src, dst, send, recv):
+        size = groups if axis == 0 else parts
+        mine = me if axis == 0 else col
+
+        def copy(s, incoming):
+            peer = (mine + s) % size
+            slot = dst(mine)
+            if incoming:
+                slot = dst((mine + size - s) % size)
+            return pltpu.make_async_remote_copy(
+                src_ref=slot if incoming else src(peer),
+                dst_ref=slot,
+                send_sem=send.at[s],
+                recv_sem=recv.at[s],
+                device_id=(peer, col) if axis == 0 else (me, peer),
+                device_id_type=MESH,
+            )
+
+        def start():
+            for s in range(1, size):
+                copy(s, False).start()
+
+        def wait():
+            for s in range(1, size):
+                copy(s, True).wait_recv()
+            for s in range(1, size):
+                copy(s, False).wait_send()
+
+        return start, wait
+
+    advance, finish = line_copies(
+        nodes.at[0], col, parts, me, cuts, line_send.at[0], line_recv.at[0]
+    )
+    start_a, wait_a = along(0, lambda p: hidden.at[me], lambda p: hidden.at[p], a_send, a_recv)
+    start_p, wait_p = along(0, lambda p: spots.at[me], lambda p: spots.at[p], p_send, p_recv)
+    start_a()
+    start_p()
+    advance(0)
+    wait_a()
+    wait_p()
+    advance(1)
+    part = jnp.dot(
+        hidden[...].reshape(groups * texts, hidden.shape[2]),
+        down[...],
+        preferred_element_type=f32,
+    )
+    share[...] = part.reshape(groups, texts, width)
+    pooled[me] = share[me]
+    start, wait = along(0, lambda p: share.at[p], lambda p: pooled.at[p], b_send, b_recv)
+    start()
+    wait()
+    terms[col] = pooled[pl.ds(col * split, split)]
+    start, wait = along(
+        1, lambda p: pooled.at[pl.ds(p * split, split)], lambda p: terms.at[p], c_send, c_recv
+    )
+    start()
+    if parts > 2:
+        advance(2)
+    wait()
+    total = jnp.zeros((texts, embed.shape[1]), f32)
+    for i in range(split):
+        value = token_mean[:, i * width : (i + 1) * width]
+        for p in range(parts):
+            value += terms[p, i]
+        high = value.astype(bf16)
+        low = (value - high.astype(f32)).astype(bf16)
+        rows = embed[i * width : (i + 1) * width, :]
+        total += jnp.dot(high, rows, preferred_element_type=f32)
+        total += jnp.dot(low, rows, preferred_element_type=f32)
+    sums[col] = total.astype(bf16)
+    start, wait = along(1, lambda p: sums.at[col], lambda p: sums.at[p], d_send, d_recv)
+    start()
+    wait()
+    total = jnp.zeros((texts, embed.shape[1]), f32)
+    for p in range(parts):
+        total += sums[p].astype(f32)
+    fresh[me] = total.astype(bf16)
+    start, wait = along(0, lambda p: fresh.at[me], lambda p: fresh.at[p], e_send, e_recv)
+    start()
+    for far in range(3, parts):
+        advance(far)
+    finish()
+    row = lax.broadcasted_iota(jnp.int32, (texts, count), 1) + me * count
+    hits = jnp.concatenate(
+        [jnp.where(row == spots[p][:, :1], 1.0, 0.0).astype(bf16) for p in range(groups)], axis=0
+    )
+    wait()
+    for p in range(parts):
+        rows = fresh[:, :, p * local : (p + 1) * local].reshape(groups * texts, local)
+        added = lax.dot_general(hits, rows, (((0,), (0,)), ((), ())), preferred_element_type=f32)
+        states[p] = (nodes[0, p].astype(f32) + added).astype(bf16)
+
+    for layer in range(layers):
+        if layer > 0:
+            advance, finish = line_copies(
+                nodes.at[layer], col, parts, me, cuts, line_send.at[layer], line_recv.at[layer]
+            )
+            for far in range(parts):
+                advance(far)
+        block = states if layer == 0 else nodes.at[layer]
+        projected = jnp.zeros((count, local), f32)
+        for p in range(parts):
+            projected += jnp.dot(
+                block[p], near_w[p * local : (p + 1) * local, :], preferred_element_type=f32
+            )
+        here = extended.at[layer]
+        here[halo : halo + count, :] = projected.astype(bf16)
+
+        @pl.when(me == 0)
+        def _():
+            here[0:halo, :] = jnp.zeros((halo, local), bf16)
+
+        @pl.when(me == groups - 1)
+        def _():
+            here[halo + count :, :] = jnp.zeros((halo, local), bf16)
+
+        def edge(way, incoming):
+            step = 1 if way == 0 else -1
+            low, high = pl.ds(0, halo), pl.ds(halo + count, halo)
+            dst = here.at[low if way == 0 else high]
+            src = here.at[pl.ds(count, halo) if way == 0 else pl.ds(halo, halo)]
+            to = me + step
+            there = (to >= 0) & (to < groups)
+            if incoming:
+                there = (me - step >= 0) & (me - step < groups)
+                src = dst
+            return there, pltpu.make_async_remote_copy(
+                src_ref=src,
+                dst_ref=dst,
+                send_sem=halo_send.at[layer, way],
+                recv_sem=halo_recv.at[layer, way],
+                device_id=(to, col),
+                device_id_type=MESH,
+            )
+
+        for way in range(2):
+            there, copy = edge(way, False)
+            pl.when(there)(copy.start)
+        if layer > 0:
+            finish()
+        near = jnp.zeros((count, local), f32)
+        for p in range(parts):
+            near += jnp.dot(
+                block[p], self_w[p * local : (p + 1) * local, :], preferred_element_type=f32
+            )
+        for way in range(2):
+            there, copy = edge(way, True)
+            pl.when(there)(copy.wait_recv)
+        near += jnp.dot(adjacency[...], here[...], preferred_element_type=f32)
+        result = jnp.maximum(near, 0.0).astype(bf16)
+        for way in range(2):
+            there, copy = edge(way, False)
+            pl.when(there)(copy.wait_send)
+        if layer < layers - 1:
+            nodes[layer + 1, col] = result
+        else:
+            out[...] = result
+
+
+def text_and_graph(
+    mean, token_mean, down, embed, place, cache, adjacency, self_w, near_w
+):
+    groups, parts = lax.axis_size("dp"), lax.axis_size("tensor")
+    texts, hidden = mean.shape
+    width, (count, local) = down.shape[1], cache.shape
+    features = embed.shape[1]
+    sem = pltpu.SemaphoreType.DMA
+    vmem = pl.BlockSpec(memory_space=pltpu.VMEM)
+    cuts = 2
+    return pl.pallas_call(
+        functools.partial(tail_kernel, groups, parts, LAYERS, cuts),
+        out_shape=jax.ShapeDtypeStruct((count, local), bf16),
+        in_specs=[vmem] * 9,
+        out_specs=vmem,
+        scratch_shapes=[
+            pltpu.VMEM((groups, texts, hidden), bf16),
+            pltpu.VMEM((groups,) + place.shape, jnp.int32),
+            pltpu.VMEM((groups, texts, width), f32),
+            pltpu.VMEM((groups, texts, width), f32),
+            pltpu.VMEM((parts, groups // parts, texts, width), f32),
+            pltpu.VMEM((parts, texts, features), bf16),
+            pltpu.VMEM((groups, texts, features), bf16),
+            pltpu.VMEM((parts, count, local), bf16),
+            pltpu.VMEM((LAYERS, parts, count, local), bf16),
+            pltpu.VMEM((LAYERS, adjacency.shape[1], local), bf16),
+        ]
+        + [sem((groups,))] * 6
+        + [sem((parts,))] * 4
+        + [sem((groups,))] * 2
+        + [sem((LAYERS, 2, parts - 1, cuts))] * 2
+        + [sem((LAYERS, 2))] * 2,
+        compiler_params=pltpu.CompilerParams(
+            collective_id=1, has_side_effects=True, vmem_limit_bytes=40 << 20
+        ),
+        name="embed_and_layers",
+    )(mean, token_mean, down, embed, place, cache, adjacency, self_w, near_w)
 
 
 def per_device(
@@ -359,15 +614,9 @@
     self_weight,
     neighbour_weight,
 ):
-    groups, parts = lax.axis_size("dp"), lax.axis_size("tensor")
-    me, col = lax.axis_index("dp"), lax.axis_index("tensor")
     text_count = text_row.shape[0]
-    texts = text_count * groups
     length = token_states.shape[0] // text_count
     node_count = node_cache.shape[0]
-    halo = BT * TILE
-
-    cache = side_by_side(spread(with_halo(node_cache, halo), "tensor"))
     row_tiles, slots = tile_index.shape
     columns = row_tiles + 2 * BT
     live = (tile_index[:, :, None] == jnp.arange(columns)[None, None, :]) & (
@@ -379,48 +628,19 @@
             live[:, slot, None, :, None], tile_weight[:, slot, :, None, :].astype(f32), 0.0
         )
     adjacency = adjacency.astype(bf16).reshape(row_tiles * TILE, columns * TILE)
-    place = text_owner[:, 0] * node_count + text_row
-    places = spread(place, "dp").reshape(-1)
-    width = down_weight.shape[1]
-    whole_embed = lax.all_gather(embed_weight, "tensor", axis=0, tiled=True)
-    own_embed = lax.dynamic_slice_in_dim(whole_embed, me * width, width, axis=0)
-    token_mean = jnp.mean(
-        token_states.astype(f32).reshape(text_count, length, -1), axis=1
-    )
-
-    mean_hidden = pooled_hidden(token_states, norm_gain, gate_weight, up_weight, length)
-
-    hidden_all = spread(mean_hidden.astype(bf16), "dp").reshape(texts, -1)
-    share = jnp.dot(hidden_all, down_weight, preferred_element_type=f32)
-    rows = texts // parts
-    part = jnp.sum(exchange(share.reshape(parts, rows, width), "tensor"), axis=0)
-    pooled = jnp.dot(part, own_embed.astype(f32), precision=lax.Precision.HIGHEST)
-    fine = rows // groups
-    pooled = jnp.sum(exchange(pooled.reshape(groups, fine, -1), "dp"), axis=0)
-    direct = jnp.dot(token_mean, embed_weight.astype(f32), precision=lax.Precision.HIGHEST)
-    direct = spread(direct, "dp").reshape(parts, rows, -1)
-    direct = jnp.sum(exchange(direct, "tensor"), axis=0)
-    direct = lax.dynamic_slice_in_dim(direct, me * fine, fine, axis=0)
-    fresh = (pooled + direct).astype(bf16)
-    fresh = spread(spread(fresh, "dp").reshape(rows, -1), "tensor").reshape(texts, -1)
-
-    ahead = me * node_count - halo + jnp.arange(cache.shape[0], dtype=jnp.int32)
-    hits = (ahead[:, None] == places[None, :]).astype(bf16)
-    added = jnp.dot(hits, fresh, preferred_element_type=f32)
-    extended = (cache.astype(f32) + added).astype(bf16)
-    gathered = extended[halo : halo + node_count]
-    for layer in range(LAYERS):
-        if layer > 0:
-            gathered = side_by_side(spread(states, "tensor"))
-            projected = jnp.dot(gathered, neighbour_weight, preferred_element_type=f32)
-            projected = with_halo(projected.astype(bf16), halo)
-        else:
-            projected = jnp.dot(extended, neighbour_weight, preferred_element_type=f32)
-            projected = projected.astype(bf16)
-        own_part = jnp.dot(gathered, self_weight, preferred_element_type=f32)
-        near_part = jnp.dot(adjacency, projected, preferred_element_type=f32)
-        states = jax.nn.relu(own_part + near_part).astype(bf16)
-    return states
+    place = jnp.broadcast_to(text_owner * node_count + text_row[:, None], (text_count, 128))
+    mean, token_mean = pooled_hidden(token_states, norm_gain, gate_weight, up_weight, length)
+    return text_and_graph(
+        mean,
+        token_mean,
+        down_weight,
+        embed_weight,
+        place,
+        node_cache,
+        adjacency,
+        self_weight,
+        neighbour_weight,
+    )
 
 
 def solution(mesh):

time: 361 us -> 152 us (0.42)
  waiting for transfers between devices: 73.6 us -> 0 us
  starting transfers between devices: 55.1 us -> 0 us
  blocking collectives: 37.7 us -> 0 us
  between operations: 13.8 us -> 0.22 us
  matrix products: 11.8 us -> 0 us
  local copies, waits for them, and re-layouts: 13.7 us -> 2.68 us
  Pallas kernels: 150 us -> 146 us
    all_to_all x8 -> x0, waiting for transfers between devices: 71.3 us -> none  [exchange(): return lax.all_to_all(block, axis, split_axis=0, concat_axis=0, tiled=True)]
    pallas_call x1, Pallas kernels: 150 us -> 82.3 us  [pooled_hidden(): pl.pallas_call(functools.partial(front_kernel, groups, parts, chunks, blo...]
    pallas_call x0 -> x1, Pallas kernels: none -> 63.9 us  [text_and_graph(): pl.pallas_call(functools.partial(tail_kernel, groups, parts, LAYERS, cuts...]
    all_to_all x8 -> x0, starting transfers between devices: 40.2 us -> none  [exchange(): return lax.all_to_all(block, axis, split_axis=0, concat_axis=0, tiled=True)]
    all_to_all x2 -> x0, blocking collectives: 37.7 us -> none  [exchange(): return lax.all_to_all(block, axis, split_axis=0, concat_axis=0, tiled=True)]
    ppermute x4 -> x0, starting transfers between devices: 14.9 us -> none  [the longest x2 10.2 us: with_halo(): high = lax.ppermute(block[:width], 'dp', backward)]
    dot_general x9 -> x0, matrix products: 11.8 us -> none  [the longest x2 4.15 us: per_device(): near_part = jnp.dot(adjacency, projected, preferred_element_type=f32)]
    broadcast_in_dim x8 -> x1, local copies, waits for them, and re-layouts: 5.27 us -> 0.07 us  [per_device(): jnp.broadcast_to(text_owner * node_count + text_row[:, None], (text_count...]
  transfers between devices with their start and end apart: 13 -> 0, of which waited for: 9 -> 0; matrix products, arithmetic and copies ran while one was open for 4% -> 0% of each run, Pallas kernels for 42% -> 0%
where the time goes in v3:
time: 152 us
  Pallas kernels  146 us (96%)
  local copies, waits for them, and re-layouts  2.68 us (2%)
  other arithmetic  2.62 us (2%)
    pallas_call x1, Pallas kernels, pooled_hidden(): pl.pallas_call(functools.partial(front_kernel, groups, parts, chunks, blo...  82.3 us
    pallas_call x1, Pallas kernels, text_and_graph(): pl.pallas_call(functools.partial(tail_kernel, groups, parts, LAYERS, cuts...  63.9 us

profile of v3, /device:TPU:1, one launch (start us, length us, event | category | flops | bytes accessed | tf_op | source)
XLA Modules:
  0.0 151.7 jit_solution(2275906314243316461)
XLA Ops:
  0.0 1.4 bitcast_convert_fusion.5
  1.4 0.0 copy-done.9
  1.4 0.1 copy.16
  1.5 0.0 copy-done.10
  1.5 0.1 copy.17
  1.6 0.1 fusion
  1.7 0.0 copy-start.8
  1.7 0.0 copy-start.7
  1.8 1.1 add_convert_fusion
  2.9 0.0 copy-start.5
  2.9 0.0 copy-start.6
  2.9 0.3 copy.23
  3.2 0.0 copy-done.8
  3.2 0.0 copy-done.7
  3.2 0.9 copy-done.5
  4.1 0.3 copy-done.6
  4.5 0.0 copy-start.2
  4.5 0.0 copy-start.3
  4.5 0.0 copy-start.4
  4.5 82.3 %gather_and_pool.1 = (f32[4,4,4,512]{3,2,1,0:T(4,128)S(1)}, f32[16,1,512]{2,1,0:T(1,128)S(1)}) custom-call(bf16[1024,512]{1,0:T(8,128)(2,1)S(1)} %copy-done.5, bf16[1,2048]{1,0:T(2,128)(2,1)S(1)} %broadcast_in_dim.103.gain, bf16[256,2048]{1,0:T(8,128)(2,1)S(1)} %copy-done.6, bf16[256,2048]{1,0:T(8,128)(2,1)S(1)} %copy-done.7), custom_call_target="tpu_custom_call" | custom-call | flops 17179869184 | bytes 16777216 | tf_op jit(solution)/shard_map/gather_and_pool/pallas_call | solution.py:300
  86.8 0.1 copy.15
  87.0 0.1 broadcast_in_dim.106.place
  87.1 63.9 %embed_and_layers.1 = bf16[512,256]{1,0:T(8,128)(2,1)S(1)} custom-call(f32[16,2048]{1,0:T(8,128)S(1)} %bitcast.49, f32[16,512]{1,0:T(8,128)S(1)} %bitcast.50, bf16[2048,256]{1,0:T(8,128)(2,1)S(1)} %copy-done, bf16[512,1024]{1,0:T(8,128)(2,1)S(1)} %copy-done.1, s32[16,128]{1,0:T(8,128)S(1)} %broadcast_in_dim.106.place, bf16[512,256]{1,0:T(8,128)(2,1)S(1)} %copy-done.4, ...), custom_call_target="tpu_custom_call" | custom-call | tf_op jit(solution)/shard_map/embed_and_layers/pallas_call | solution.py:572
  151.0 0.7 copy.26
  (19 shorter events, 0.1 us)
Async XLA Ops:
  0.0 1.4 copy-start.9
  0.0 1.5 copy-start.10
  1.7 1.5 copy-start.8
  1.7 1.5 copy-start.7
  2.9 1.2 copy-start.5
  2.9 1.5 %copy-start.6 = (bf16[256,2048]{1,0:T(8,128)(2,1)S(1)}, bf16[256,2048]{1,0:T(8,128)(2,1)}, u32[]{:S(2)}) copy-start(bf16[256,2048]{1,0:T(8,128)(2,1)} %gw.1) | copy-start | bytes 3145732
  4.5 82.5 %copy-start.11 = (s32[16]{0:T(128)S(1)}, s32[16]{0:T(128)}, u32[]{:S(2)}) copy-start(s32[16]{0:T(128)} %param.21) | copy-start | bytes 196
  4.5 82.5 %copy-start.12 = (s32[16,1]{0,1:T(1,128)S(1)}, s32[16,1]{0,1:T(1,128)}, u32[]{:S(2)}) copy-start(s32[16,1]{0,1:T(1,128)} %param.20) | copy-start | bytes 196
  4.5 82.6 %copy-start = (bf16[2048,256]{1,0:T(8,128)(2,1)S(1)}, bf16[2048,256]{1,0:T(8,128)(2,1)}, u32[]{:S(2)}) copy-start(bf16[2048,256]{1,0:T(8,128)(2,1)} %down.1) | copy-start | bytes 3145732
  4.5 82.6 %copy-start.1 = (bf16[512,1024]{1,0:T(8,128)(2,1)S(1)}, bf16[512,1024]{1,0:T(8,128)(2,1)}, u32[]{:S(2)}) copy-start(bf16[512,1024]{1,0:T(8,128)(2,1)} %embed.1) | copy-start | bytes 3145732
  4.5 82.6 %copy-start.2 = (bf16[1024,256]{1,0:T(8,128)(2,1)S(1)}, bf16[1024,256]{1,0:T(8,128)(2,1)}, u32[]{:S(2)}) copy-start(bf16[1024,256]{1,0:T(8,128)(2,1)} %self_w.1) | copy-start | bytes 1572868
  4.5 82.6 %copy-start.3 = (bf16[1024,256]{1,0:T(8,128)(2,1)S(1)}, bf16[1024,256]{1,0:T(8,128)(2,1)}, u32[]{:S(2)}) copy-start(bf16[1024,256]{1,0:T(8,128)(2,1)} %near_w.1) | copy-start | bytes 1572868
  4.5 82.6 %copy-start.4 = (bf16[512,256]{1,0:T(8,128)(2,1)S(1)}, bf16[512,256]{1,0:T(8,128)(2,1)}, u32[]{:S(2)}) copy-start(bf16[512,256]{1,0:T(8,128)(2,1)} %cache.1) | copy-start | bytes 786436

commit v4 on v3

--- a/solution.py
+++ b/solution.py
@@ -7,7 +7,6 @@
 from jax.experimental.pallas import tpu as pltpu
 from jax.sharding import PartitionSpec as P
 
-TILE = 128
 BT = 2
 LAYERS = 2
 
@@ -80,7 +79,7 @@
 
 
 def front_kernel(
-    groups, parts, chunks, blocks, length, bits, hops, cube,
+    groups, parts, chunks, blocks, merge, length, bits, hops, cube,
     tok, gain, gw, uw, out, own_mean, whole, normed, gfull, ufull,
     hop_send, hop_recv, cube_send, cube_recv, pair_send, pair_recv, own_sem,
 ):
@@ -191,17 +190,18 @@
         lax.fori_loop(0, rows // length, one, 0)
 
     def work(block, chunk):
-        x = normed[pl.ds(pl.multiple_of(block * rows, rows), rows), :]
+        tall = rows * merge
+        x = normed[pl.ds(pl.multiple_of(block * tall, tall), tall), :]
         gate = jnp.dot(x, gfull[chunk], preferred_element_type=f32)
         upward = jnp.dot(x, ufull[chunk], preferred_element_type=f32)
         hidden = (gate / (1.0 + jnp.exp(-gate)) * upward).astype(bf16).astype(f32)
-        mean = jnp.sum(hidden.reshape(rows // length, length, width), axis=1)
+        mean = jnp.sum(hidden.reshape(tall // length, length, width), axis=1)
         out[chunk, block] = mean * (1.0 / length)
 
     turns = max([len(hops)] + [len(cube[bit]) for bit in bits])
     missing = {chunk: 2 * groups for chunk in range(chunks)}
     unhopped = {block: parts - 1 for block in range(blocks)}
-    ready_chunks, ready_blocks = [], []
+    ready_chunks, ready_blocks, came = [], [], []
     flying = []
 
     for array in range(2):
@@ -256,6 +256,10 @@
                 missing[chunk] -= 2
         for block in new_blocks:
             normalise(block)
+            came.append(block)
+            block = block // merge
+            if not all(block * merge + n in came for n in range(merge)):
+                continue
             if ready_chunks:
                 def across(n, _, block=block):
                     work(block, n)
@@ -279,14 +283,15 @@
                         return 0
                     lax.fori_loop(0, len(ready_blocks), down, 0)
                 ready_chunks.append(chunk)
-    assert len(ready_chunks) == chunks and len(ready_blocks) == blocks and not flying
+    assert len(ready_chunks) == chunks and len(ready_blocks) == blocks // merge and not flying
 
 
 def pooled_hidden(token_states, norm_gain, gate_weight, up_weight, length):
     groups, parts = lax.axis_size("dp"), lax.axis_size("tensor")
     tokens, local = token_states.shape
     depth, hidden = gate_weight.shape
-    chunks = blocks = 4
+    chunks = blocks = 8
+    merge = 2
     width, rows = hidden // chunks, tokens // blocks
     bits = [1 << n for n in range(1, (groups - 1).bit_length())]
     hops = hop_plan(blocks, parts - 1)
@@ -299,10 +304,10 @@
     vmem = pl.BlockSpec(memory_space=pltpu.VMEM)
     mean, own_mean = pl.pallas_call(
         functools.partial(
-            front_kernel, groups, parts, chunks, blocks, length, bits, hops, cube
+            front_kernel, groups, parts, chunks, blocks, merge, length, bits, hops, cube
         ),
         out_shape=[
-            jax.ShapeDtypeStruct((chunks, blocks, rows // length, width), f32),
+            jax.ShapeDtypeStruct((chunks, blocks // merge, rows * merge // length, width), f32),
             jax.ShapeDtypeStruct((tokens // length, 1, local), f32),
         ],
         in_specs=[any_space, vmem, any_space, any_space],
@@ -375,8 +380,8 @@
 
 def tail_kernel(
     groups, parts, layers, cuts,
-    mean, token_mean, down, embed, place, cache, adjacency, self_w, near_w, out,
-    hidden, spots, share, pooled, terms, sums, fresh, states, nodes, extended,
+    mean, token_mean, down, embed, place, cache, index, live, tiles, self_w, near_w, out,
+    adjacency, hidden, spots, share, pooled, terms, sums, fresh, states, nodes, extended,
     a_send, a_recv, p_send, p_recv, b_send, b_recv, c_send, c_recv,
     d_send, d_recv, e_send, e_recv, line_send, line_recv, halo_send, halo_recv,
 ):
@@ -438,6 +443,19 @@
     start_a()
     start_p()
     advance(0)
+    row_tiles, slots, tile = tiles.shape[0], tiles.shape[1], tiles.shape[2]
+
+    def fill(r, _):
+        rows = pl.ds(pl.multiple_of(r * tile, tile), tile)
+        for c in range(adjacency.shape[1] // tile):
+            total = jnp.zeros((tile, tile), f32)
+            for k in range(slots):
+                weight = jnp.where(index[r, k] == c, live[r, k], 0).astype(f32)
+                total += weight * tiles[r, k].astype(f32)
+            adjacency[rows, c * tile : (c + 1) * tile] = total.astype(bf16)
+        return 0
+
+    lax.fori_loop(0, row_tiles, fill, 0)
     wait_a()
     wait_p()
     advance(1)
@@ -560,7 +578,7 @@
 
 
 def text_and_graph(
-    mean, token_mean, down, embed, place, cache, adjacency, self_w, near_w
+    mean, token_mean, down, embed, place, cache, index, live, tiles, self_w, near_w
 ):
     groups, parts = lax.axis_size("dp"), lax.axis_size("tensor")
     texts, hidden = mean.shape
@@ -569,12 +587,15 @@
     sem = pltpu.SemaphoreType.DMA
     vmem = pl.BlockSpec(memory_space=pltpu.VMEM)
     cuts = 2
+    smem = pl.BlockSpec(memory_space=pltpu.SMEM)
+    reach = count + 2 * BT * tiles.shape[2]
     return pl.pallas_call(
         functools.partial(tail_kernel, groups, parts, LAYERS, cuts),
         out_shape=jax.ShapeDtypeStruct((count, local), bf16),
-        in_specs=[vmem] * 9,
+        in_specs=[vmem] * 6 + [smem] * 2 + [vmem] * 3,
         out_specs=vmem,
         scratch_shapes=[
+            pltpu.VMEM((count, reach), bf16),
             pltpu.VMEM((groups, texts, hidden), bf16),
             pltpu.VMEM((groups,) + place.shape, jnp.int32),
             pltpu.VMEM((groups, texts, width), f32),
@@ -584,7 +605,7 @@
             pltpu.VMEM((groups, texts, features), bf16),
             pltpu.VMEM((parts, count, local), bf16),
             pltpu.VMEM((LAYERS, parts, count, local), bf16),
-            pltpu.VMEM((LAYERS, adjacency.shape[1], local), bf16),
+            pltpu.VMEM((LAYERS, reach, local), bf16),
         ]
         + [sem((groups,))] * 6
         + [sem((parts,))] * 4
@@ -595,7 +616,7 @@
             collective_id=1, has_side_effects=True, vmem_limit_bytes=40 << 20
         ),
         name="embed_and_layers",
-    )(mean, token_mean, down, embed, place, cache, adjacency, self_w, near_w)
+    )(mean, token_mean, down, embed, place, cache, index, live, tiles, self_w, near_w)
 
 
 def per_device(
@@ -617,17 +638,6 @@
     text_count = text_row.shape[0]
     length = token_states.shape[0] // text_count
     node_count = node_cache.shape[0]
-    row_tiles, slots = tile_index.shape
-    columns = row_tiles + 2 * BT
-    live = (tile_index[:, :, None] == jnp.arange(columns)[None, None, :]) & (
-        tile_live[:, :, None] != 0
-    )
-    adjacency = jnp.zeros((row_tiles, TILE, columns, TILE), f32)
-    for slot in range(slots):
-        adjacency += jnp.where(
-            live[:, slot, None, :, None], tile_weight[:, slot, :, None, :].astype(f32), 0.0
-        )
-    adjacency = adjacency.astype(bf16).reshape(row_tiles * TILE, columns * TILE)
     place = jnp.broadcast_to(text_owner * node_count + text_row[:, None], (text_count, 128))
     mean, token_mean = pooled_hidden(token_states, norm_gain, gate_weight, up_weight, length)
     return text_and_graph(
@@ -637,7 +647,9 @@
         embed_weight,
         place,
         node_cache,
-        adjacency,
+        tile_index,
+        tile_live,
+        tile_weight,
         self_weight,
         neighbour_weight,
     )

time: 152 us -> 157 us (1.033)
  local copies, waits for them, and re-layouts: 2.68 us -> 6.05 us
  Pallas kernels: 146 us -> 149 us
  other arithmetic: 2.62 us -> 0.67 us
    unnamed x31 -> x27, local copies, waits for them, and re-layouts: 2.4 us -> 5.89 us
    pallas_call x1, Pallas kernels: 82.3 us -> 85.4 us  [pooled_hidden(): pl.pallas_call(functools.partial(front_kernel, groups, parts, chunks, blo...]
    convert_element_type x2 -> x0, other arithmetic: 2.53 us -> none  [the longest x1 1.39 us: per_device(): tile_weight[:, slot, :, None, :].astype(f32)]
where the time goes in v4:
time: 157 us; the launch traced here: 156 us
  Pallas kernels  149 us (95%)
  local copies, waits for them, and re-layouts  6.05 us (4%)
    pallas_call x1, Pallas kernels, pooled_hidden(): pl.pallas_call(functools.partial(front_kernel, groups, parts, chunks, blo...  85.4 us
    pallas_call x1, Pallas kernels, text_and_graph(): pl.pallas_call(functools.partial(tail_kernel, groups, parts, LAYERS, cuts...  63.9 us
    unnamed x27, local copies, waits for them, and re-layouts  5.89 us

profile of v4, /device:TPU:1, one launch (start us, length us, event | category | flops | bytes accessed | tf_op | source)
XLA Modules:
  0.0 156.2 jit_solution(11124591444699756200)
XLA Ops:
  0.0 0.7 fusion
  0.7 0.0 copy-start.11
  0.7 0.1 broadcast_in_dim.16.place
  0.7 0.6 copy-done.11
  1.4 0.0 copy-start.8
  1.4 1.2 copy-done.8
  2.6 1.2 copy-done.9
  3.8 1.2 copy-done.10
  5.1 0.0 copy-start.5
  5.1 0.0 copy-start.6
  5.1 0.0 copy-start.7
  5.1 85.4 %gather_and_pool.1 = (f32[8,4,4,256]{3,2,1,0:T(4,128)S(1)}, f32[16,1,512]{2,1,0:T(1,128)S(1)}) custom-call(bf16[1024,512]{1,0:T(8,128)(2,1)S(1)} %copy-done.8, bf16[1,2048]{1,0:T(2,128)(2,1)S(1)} %broadcast_in_dim.13.gain, bf16[256,2048]{1,0:T(8,128)(2,1)S(1)} %copy-done.9, bf16[256,2048]{1,0:T(8,128)(2,1)S(1)} %copy-done.10), custom_call_target="tpu_custom_call" | custom-call | flops 17179869184 | bytes 16777216 | tf_op jit(solution)/shard_map/gather_and_pool/pallas_call | solution.py:305
  90.5 0.0 copy-start.3
  90.5 0.1 copy.15
  90.7 0.0 copy-done
  90.7 0.0 copy-done.1
  90.7 0.0 copy-done.2
  90.7 0.0 copy-done.4
  90.7 0.0 copy-done.5
  90.7 0.0 copy-done.6
  90.7 0.0 copy-done.7
  90.8 0.8 copy-done.3
  91.6 63.9 %embed_and_layers.1 = bf16[512,256]{1,0:T(8,128)(2,1)S(1)} custom-call(f32[16,2048]{1,0:T(8,128)S(1)} %bitcast.13, f32[16,512]{1,0:T(8,128)S(1)} %bitcast.14, bf16[2048,256]{1,0:T(8,128)(2,1)S(1)} %copy-done, bf16[512,1024]{1,0:T(8,128)(2,1)S(1)} %copy-done.1, s32[16,128]{1,0:T(8,128)S(1)} %broadcast_in_dim.16.place, bf16[512,256]{1,0:T(8,128)(2,1)S(1)} %copy-done.5, ...), custom_call_target="tpu_custom_call" | custom-call | tf_op jit(solution)/shard_map/embed_and_layers/pallas_call | solution.py:592
  155.5 0.7 copy.21
  (9 shorter events, 0.1 us)
Async XLA Ops:
  0.7 0.7 copy-start.11
  1.4 1.2 copy-start.8
  2.6 1.2 copy-start.9
  3.8 1.2 copy-start.10
  5.0 85.6 %copy-start = (bf16[2048,256]{1,0:T(8,128)(2,1)S(1)}, bf16[2048,256]{1,0:T(8,128)(2,1)}, u32[]{:S(2)}) copy-start(bf16[2048,256]{1,0:T(8,128)(2,1)} %down.1) | copy-start | bytes 3145732
  5.0 85.6 %copy-start.1 = (bf16[512,1024]{1,0:T(8,128)(2,1)S(1)}, bf16[512,1024]{1,0:T(8,128)(2,1)}, u32[]{:S(2)}) copy-start(bf16[512,1024]{1,0:T(8,128)(2,1)} %embed.1) | copy-start | bytes 3145732
  5.1 85.7 %copy-start.2 = (bf16[4,6,128,128]{3,2,1,0:T(8,128)(2,1)S(1)}, bf16[4,6,128,128]{3,2,1,0:T(8,128)(2,1)}, u32[]{:S(2)}) copy-start(bf16[4,6,128,128]{3,2,1,0:T(8,128)(2,1)} %tiles.1) | copy-start | bytes 2359300
  5.1 85.7 %copy-start.4 = (bf16[1024,256]{1,0:T(8,128)(2,1)S(1)}, bf16[1024,256]{1,0:T(8,128)(2,1)}, u32[]{:S(2)}) copy-start(bf16[1024,256]{1,0:T(8,128)(2,1)} %near_w.1) | copy-start | bytes 1572868
  5.1 85.7 %copy-start.5 = (bf16[512,256]{1,0:T(8,128)(2,1)S(1)}, bf16[512,256]{1,0:T(8,128)(2,1)}, u32[]{:S(2)}) copy-start(bf16[512,256]{1,0:T(8,128)(2,1)} %cache.1) | copy-start | bytes 786436
  5.1 85.7 %copy-start.6 = (s32[4,6]{1,0:T(4,128)S(1)}, s32[4,6]{1,0:T(4,128)}, u32[]{:S(2)}) copy-start(s32[4,6]{1,0:T(4,128)} %index.1) | copy-start | bytes 292
  5.1 85.7 %copy-start.7 = (s32[4,6]{1,0:T(4,128)S(1)}, s32[4,6]{1,0:T(4,128)}, u32[]{:S(2)}) copy-start(s32[4,6]{1,0:T(4,128)} %live.1) | copy-start | bytes 292
  90.5 1.0 copy-start.3

commit v5 on v3

--- a/solution.py
+++ b/solution.py
@@ -7,7 +7,6 @@
 from jax.experimental.pallas import tpu as pltpu
 from jax.sharding import PartitionSpec as P
 
-TILE = 128
 BT = 2
 LAYERS = 2
 
@@ -80,9 +79,9 @@
 
 
 def front_kernel(
-    groups, parts, chunks, blocks, length, bits, hops, cube,
-    tok, gain, gw, uw, out, own_mean, whole, normed, gfull, ufull,
-    hop_send, hop_recv, cube_send, cube_recv, pair_send, pair_recv, own_sem,
+    groups, parts, chunks, blocks, merge, length, bits, hops, cube,
+    tok, gain, gw, uw, index, live, stored, out, own_mean, adjacency, whole, normed, gfull, ufull,
+    hop_send, hop_recv, cube_send, cube_recv, pair_send, pair_recv, own_sem, tiles,
 ):
     me, col = lax.axis_index("dp"), lax.axis_index("tensor")
     depth, width = gw.shape[0], gfull.shape[2]
@@ -112,6 +111,7 @@
                     own_sem.at[1 + array * chunks + chunk],
                 )
             )
+    own.append(pltpu.make_async_copy(stored, tiles, own_sem.at[1 + 2 * chunks]))
     for copy in own:
         copy.start()
 
@@ -190,18 +190,20 @@
 
         lax.fori_loop(0, rows // length, one, 0)
 
-    def work(block, chunk):
-        x = normed[pl.ds(pl.multiple_of(block * rows, rows), rows), :]
+    def work(block, chunk, many=1):
+        tall = rows * merge * many
+        x = normed[pl.ds(pl.multiple_of(block * rows * merge, rows), tall), :]
         gate = jnp.dot(x, gfull[chunk], preferred_element_type=f32)
         upward = jnp.dot(x, ufull[chunk], preferred_element_type=f32)
         hidden = (gate / (1.0 + jnp.exp(-gate)) * upward).astype(bf16).astype(f32)
-        mean = jnp.sum(hidden.reshape(rows // length, length, width), axis=1)
-        out[chunk, block] = mean * (1.0 / length)
+        mean = jnp.sum(hidden.reshape(tall // length, length, width), axis=1)
+        mean = (mean * (1.0 / length)).reshape((many,) + out.shape[2:])
+        out[chunk, pl.ds(block, many)] = mean
 
     turns = max([len(hops)] + [len(cube[bit]) for bit in bits])
     missing = {chunk: 2 * groups for chunk in range(chunks)}
     unhopped = {block: parts - 1 for block in range(blocks)}
-    ready_chunks, ready_blocks = [], []
+    ready_chunks, ready_blocks, came = [], [], []
     flying = []
 
     for array in range(2):
@@ -252,10 +254,27 @@
                 return 0
 
             lax.fori_loop(0, tok.shape[0] // length, average, 0)
+            row_tiles, slots, tile = tiles.shape[0], tiles.shape[1], tiles.shape[2]
+
+            def fill(r, _):
+                rows = pl.ds(pl.multiple_of(r * tile, tile), tile)
+                for c in range(adjacency.shape[1] // tile):
+                    total = jnp.zeros((tile, tile), f32)
+                    for k in range(slots):
+                        weight = jnp.where(index[r, k] == c, live[r, k], 0).astype(f32)
+                        total += weight * tiles[r, k].astype(f32)
+                    adjacency[rows, c * tile : (c + 1) * tile] = total.astype(bf16)
+                return 0
+
+            lax.fori_loop(0, row_tiles, fill, 0)
             for chunk in range(chunks):
                 missing[chunk] -= 2
         for block in new_blocks:
             normalise(block)
+            came.append(block)
+            block = block // merge
+            if not all(block * merge + n in came for n in range(merge)):
+                continue
             if ready_chunks:
                 def across(n, _, block=block):
                     work(block, n)
@@ -275,18 +294,23 @@
                 if ready_blocks:
                     assert ready_blocks == list(range(len(ready_blocks)))
                     def down(n, _, chunk=chunk):
-                        work(n, chunk)
+                        work(2 * n, chunk, 2)
                         return 0
-                    lax.fori_loop(0, len(ready_blocks), down, 0)
+                    lax.fori_loop(0, len(ready_blocks) // 2, down, 0)
+                    if len(ready_blocks) % 2:
+                        work(len(ready_blocks) - 1, chunk)
                 ready_chunks.append(chunk)
-    assert len(ready_chunks) == chunks and len(ready_blocks) == blocks and not flying
-
-
-def pooled_hidden(token_states, norm_gain, gate_weight, up_weight, length):
+    assert len(ready_chunks) == chunks and len(ready_blocks) == blocks // merge and not flying
+
+
+def pooled_hidden(
+    token_states, norm_gain, gate_weight, up_weight, index, live, tile_weight, length
+):
     groups, parts = lax.axis_size("dp"), lax.axis_size("tensor")
     tokens, local = token_states.shape
     depth, hidden = gate_weight.shape
     chunks = blocks = 4
+    merge = 1
     width, rows = hidden // chunks, tokens // blocks
     bits = [1 << n for n in range(1, (groups - 1).bit_length())]
     hops = hop_plan(blocks, parts - 1)
@@ -295,18 +319,22 @@
     pairs = 2 * chunks * (groups // 2)
     sem = pltpu.SemaphoreType.DMA
     features = parts * local
-    any_space = pl.BlockSpec(memory_space=pl.ANY)
+    hbm = pl.BlockSpec(memory_space=pltpu.HBM)
+    smem = pl.BlockSpec(memory_space=pltpu.SMEM)
+    row_tiles, _, tile, _ = tile_weight.shape
+    nodes = row_tiles * tile
     vmem = pl.BlockSpec(memory_space=pltpu.VMEM)
-    mean, own_mean = pl.pallas_call(
+    mean, own_mean, adjacency = pl.pallas_call(
         functools.partial(
-            front_kernel, groups, parts, chunks, blocks, length, bits, hops, cube
+            front_kernel, groups, parts, chunks, blocks, merge, length, bits, hops, cube
         ),
         out_shape=[
-            jax.ShapeDtypeStruct((chunks, blocks, rows // length, width), f32),
+            jax.ShapeDtypeStruct((chunks, blocks // merge, rows * merge // length, width), f32),
             jax.ShapeDtypeStruct((tokens // length, 1, local), f32),
+            jax.ShapeDtypeStruct((nodes, nodes + 2 * BT * tile), bf16),
         ],
-        in_specs=[any_space, vmem, any_space, any_space],
-        out_specs=[vmem, vmem],
+        in_specs=[hbm, vmem, hbm, hbm, smem, smem, hbm],
+        out_specs=[vmem, vmem, vmem],
         scratch_shapes=[
             pltpu.VMEM((parts, tokens, local), bf16),
             pltpu.VMEM((tokens, features), bf16),
@@ -318,10 +346,11 @@
             sem((len(bits), turns)),
             sem((pairs,)),
             sem((pairs,)),
-            sem((1 + 2 * chunks,)),
+            sem((2 + 2 * chunks,)),
+            pltpu.VMEM(tile_weight.shape, bf16),
         ],
         compiler_params=pltpu.CompilerParams(
-            collective_id=0, has_side_effects=True, vmem_limit_bytes=48 << 20
+            collective_id=0, has_side_effects=True, vmem_limit_bytes=56 << 20
         ),
         cost_estimate=pl.CostEstimate(
             flops=4 * tokens * features * hidden,
@@ -329,9 +358,9 @@
             transcendentals=tokens * hidden,
         ),
         name="gather_and_pool",
-    )(token_states, norm_gain[None], gate_weight, up_weight)
+    )(token_states, norm_gain[None], gate_weight, up_weight, index, live, tile_weight)
     mean = jnp.transpose(mean, (1, 2, 0, 3)).reshape(tokens // length, hidden)
-    return mean, own_mean[:, 0]
+    return mean, own_mean[:, 0], adjacency
 
 
 def line_copies(buffer, col, parts, me, cuts, send, recv):
@@ -569,6 +598,7 @@
     sem = pltpu.SemaphoreType.DMA
     vmem = pl.BlockSpec(memory_space=pltpu.VMEM)
     cuts = 2
+    reach = adjacency.shape[1]
     return pl.pallas_call(
         functools.partial(tail_kernel, groups, parts, LAYERS, cuts),
         out_shape=jax.ShapeDtypeStruct((count, local), bf16),
@@ -584,7 +614,7 @@
             pltpu.VMEM((groups, texts, features), bf16),
             pltpu.VMEM((parts, count, local), bf16),
             pltpu.VMEM((LAYERS, parts, count, local), bf16),
-            pltpu.VMEM((LAYERS, adjacency.shape[1], local), bf16),
+            pltpu.VMEM((LAYERS, reach, local), bf16),
         ]
         + [sem((groups,))] * 6
         + [sem((parts,))] * 4
@@ -617,19 +647,10 @@
     text_count = text_row.shape[0]
     length = token_states.shape[0] // text_count
     node_count = node_cache.shape[0]
-    row_tiles, slots = tile_index.shape
-    columns = row_tiles + 2 * BT
-    live = (tile_index[:, :, None] == jnp.arange(columns)[None, None, :]) & (
-        tile_live[:, :, None] != 0
-    )
-    adjacency = jnp.zeros((row_tiles, TILE, columns, TILE), f32)
-    for slot in range(slots):
-        adjacency += jnp.where(
-            live[:, slot, None, :, None], tile_weight[:, slot, :, None, :].astype(f32), 0.0
-        )
-    adjacency = adjacency.astype(bf16).reshape(row_tiles * TILE, columns * TILE)
     place = jnp.broadcast_to(text_owner * node_count + text_row[:, None], (text_count, 128))
-    mean, token_mean = pooled_hidden(token_states, norm_gain, gate_weight, up_weight, length)
+    mean, token_mean, adjacency = pooled_hidden(
+        token_states, norm_gain, gate_weight, up_weight, tile_index, tile_live, tile_weight, length
+    )
     return text_and_graph(
         mean,
         token_mean,

time: 152 us -> 154 us (1.013)
  local copies, waits for them, and re-layouts: 2.68 us -> 5.09 us
  Pallas kernels: 146 us -> 148 us
  other arithmetic: 2.62 us -> 0.67 us
    convert_element_type x2 -> x0, other arithmetic: 2.53 us -> none  [the longest x1 1.39 us: per_device(): tile_weight[:, slot, :, None, :].astype(f32)]
    pallas_call x1, Pallas kernels: 82.3 us -> 84.2 us  [pooled_hidden(): pl.pallas_call(functools.partial(front_kernel, groups, parts, chunks, blo...]
    unnamed x31 -> x17, local copies, waits for them, and re-layouts: 2.4 us -> 3.37 us
where the time goes in v5:
time: 154 us
  Pallas kernels  148 us (96%)
  local copies, waits for them, and re-layouts  5.09 us (3%)
    pallas_call x1, Pallas kernels, pooled_hidden(): pl.pallas_call(functools.partial(front_kernel, groups, parts, chunks, blo...  84.2 us
    pallas_call x1, Pallas kernels, text_and_graph(): pl.pallas_call(functools.partial(tail_kernel, groups, parts, LAYERS, cuts...  63.6 us
    unnamed x17, local copies, waits for them, and re-layouts  3.37 us

profile of v5, /device:TPU:1, one launch (start us, length us, event | category | flops | bytes accessed | tf_op | source)
XLA Modules:
  0.0 153.6 jit_solution(7289029198580547047)
XLA Ops:
  0.0 0.7 fusion
  0.7 0.0 copy-start.6
  0.7 0.1 broadcast_in_dim.16.place
  0.7 0.6 copy-done.6
  1.4 0.6 broadcast_in_dim.13.gain
  2.0 0.0 copy-start
  2.0 0.0 copy-start.1
  2.0 0.0 copy-start.4
  2.0 0.0 copy-start.5
  2.0 84.2 %gather_and_pool.1 = (f32[4,4,4,512]{3,2,1,0:T(4,128)}, f32[16,1,512]{2,1,0:T(1,128)}, bf16[512,1024]{1,0:T(8,128)(2,1)}) custom-call(bf16[1024,512]{1,0:T(8,128)(2,1)} %tok.1, bf16[1,2048]{1,0:T(2,128)(2,1)} %broadcast_in_dim.13.gain, bf16[256,2048]{1,0:T(8,128)(2,1)} %gw.1, bf16[256,2048]{1,0:T(8,128)(2,1)} %uw.1, s32[4,6]{1,0:T(4,128)} %index.1, ...), custom_call_target="tpu_custom_call" | custom-call | flops 17179869184 | bytes 16777216 | tf_op jit(solution)/shard_map/gather_and_pool/pallas_call | solution.py:327
  86.2 0.0 copy-start.3
  86.2 1.0 copy.15
  87.3 0.8 copy.19
  88.1 0.0 copy-done
  88.1 0.0 copy-done.1
  88.1 0.0 copy-done.4
  88.1 0.0 copy-done.5
  88.1 0.0 copy-done.3
  88.1 0.0 copy-start.2
  88.1 1.2 copy-done.2
  89.3 63.6 %embed_and_layers.1 = bf16[512,256]{1,0:T(8,128)(2,1)S(1)} custom-call(f32[16,2048]{1,0:T(8,128)S(1)} %bitcast.13, f32[16,512]{1,0:T(8,128)S(1)} %bitcast.14, bf16[2048,256]{1,0:T(8,128)(2,1)S(1)} %copy-done, bf16[512,1024]{1,0:T(8,128)(2,1)S(1)} %copy-done.1, s32[16,128]{1,0:T(8,128)S(1)} %broadcast_in_dim.16.place, bf16[512,256]{1,0:T(8,128)(2,1)S(1)} %copy-done.5, ...), custom_call_target="tpu_custom_call" | custom-call | tf_op jit(solution)/shard_map/embed_and_layers/pallas_call | solution.py:602
  152.9 0.7 copy.21
  (1 shorter events, 0.0 us)
Async XLA Ops:
  0.7 0.7 copy-start.6
  2.0 86.1 %copy-start = (bf16[2048,256]{1,0:T(8,128)(2,1)S(1)}, bf16[2048,256]{1,0:T(8,128)(2,1)}, u32[]{:S(2)}) copy-start(bf16[2048,256]{1,0:T(8,128)(2,1)} %down.1) | copy-start | bytes 3145732
  2.0 86.1 %copy-start.1 = (bf16[512,1024]{1,0:T(8,128)(2,1)S(1)}, bf16[512,1024]{1,0:T(8,128)(2,1)}, u32[]{:S(2)}) copy-start(bf16[512,1024]{1,0:T(8,128)(2,1)} %embed.1) | copy-start | bytes 3145732
  2.0 86.1 %copy-start.4 = (bf16[1024,256]{1,0:T(8,128)(2,1)S(1)}, bf16[1024,256]{1,0:T(8,128)(2,1)}, u32[]{:S(2)}) copy-start(bf16[1024,256]{1,0:T(8,128)(2,1)} %near_w.1) | copy-start | bytes 1572868
  2.0 86.1 %copy-start.5 = (bf16[512,256]{1,0:T(8,128)(2,1)S(1)}, bf16[512,256]{1,0:T(8,128)(2,1)}, u32[]{:S(2)}) copy-start(bf16[512,256]{1,0:T(8,128)(2,1)} %cache.1) | copy-start | bytes 786436
  86.2 1.9 %copy-start.3 = (bf16[1024,256]{1,0:T(8,128)(2,1)S(1)}, bf16[1024,256]{1,0:T(8,128)(2,1)}, u32[]{:S(2)}) copy-start(bf16[1024,256]{1,0:T(8,128)(2,1)} %self_w.1) | copy-start | bytes 1572868
  88.1 1.2 copy-start.2
